TPU v7x, 256 devices: a whole 4x4x8 slice. The times are simulated.
256 devices in a mesh: strike: 32 (over z, y_hi, core), cross: 8 (over x, y_lo).
Axes of the slice: x: 4, y: 4 (y_hi: 2, y_lo: 2; y = y_hi * 2 + y_lo), z: 8, core: 2. Of those that a mesh axis runs over, the one named last changes fastest.
Arguments:
- velocity: float32 [3, 512, 128, 256], P(None, 'strike', 'cross'), may hold values from -4 to 4
- stress: float32 [6, 512, 128, 256], P(None, 'strike', 'cross'), may hold values from -1.6 to 1.6
- buoyancy: float32 [512, 128, 256], P('strike', 'cross'), may hold values from 0.5 to 1
- lame: float32 [512, 128, 256], P('strike', 'cross'), may hold values from 0.5 to 1.2
- shear: float32 [512, 128, 256], P('strike', 'cross'), may hold values from 0.5 to 1
- fault_tile: int32 [32], replicated, may hold values from 1 to 7
- prestress: float32 [512, 256], P('strike', 'cross'), may hold values from 1.2 to 2.4
- normal_stress: float32 [512, 256], P('strike', 'cross'), may hold values from 2 to 4
- rate_a: float32 [512, 256], P('strike', 'cross'), may hold values from 0.02 to 0.04
- state: float32 [512, 256], P('strike', 'cross'), may hold values from 0.45 to 0.6
Outputs:
- velocity_out: float32 [3, 512, 128, 256], P(None, 'strike', 'cross')
- stress_out: float32 [6, 512, 128, 256], P(None, 'strike', 'cross')
- slip_rate: float32 [512, 256], P('strike', 'cross')
- state_out: float32 [512, 256], P('strike', 'cross')
Inputs may be any that keep to these rules, and one draw needn't show every extreme that they name: `fault_tile`: each strike index has its fault plane in the first row of one cross tile other than the first.
All inputs are finite; a program needn't handle non-finite values.
Results may differ from a plain program's by a relative error of at most 0.0003.
Values sent between devices are 32-bit elements; how exact they have to be, the bound alone decides.
A program may use at most 64 MiB of HBM per device.

v0:
```python
import jax
import jax.numpy as jnp
from jax import lax
from jax.sharding import PartitionSpec as P

STEPS = 4
NEWTON = 8


step_ratio = 0.25
ref_rate = 0.001
evolve_rate = 1e-05
base_friction = 0.6
evolve_b = 0.03


def with_halo(shard, sides, width):
    for axis, dim in sides:
        size, length = (lax.axis_size(axis), shard.shape[dim])
        up = [(i, (i + 1) % size) for i in range(size - 1)]
        down = [(j, i) for i, j in up]
        last = lax.slice_in_dim(shard, length - width, length, axis=dim)
        first = lax.slice_in_dim(shard, 0, width, axis=dim)
        before = lax.ppermute(last, axis, up)
        after = lax.ppermute(first, axis, down)
        shard = jnp.concatenate([before, shard, after], axis=dim)
    return shard


def inverse_sinh(value):
    magnitude = jnp.abs(value)
    return jnp.sign(value) * jnp.log(magnitude + jnp.sqrt(magnitude * magnitude + 1.0))


def shifted(field, axis_pos, offset):
    parts = [slice(2, field.shape[position] - 2) for position in range(3)]
    parts[axis_pos] = slice(2 + offset, field.shape[axis_pos] - 2 + offset)
    return field[tuple(parts)]


def forward_diff(field, axis_pos):
    return (
        1.125 * (shifted(field, axis_pos, 1) - shifted(field, axis_pos, 0))
        - (shifted(field, axis_pos, 2) - shifted(field, axis_pos, -1)) / 24.0
    )


def backward_diff(field, axis_pos):
    return (
        1.125 * (shifted(field, axis_pos, 0) - shifted(field, axis_pos, -1))
        - (shifted(field, axis_pos, 1) - shifted(field, axis_pos, -2)) / 24.0
    )


def velocity_update(velocity, padded, buoyancy):
    strike_force = (
        forward_diff(padded[0], 0) + backward_diff(padded[3], 1) + backward_diff(padded[4], 2)
    )
    cross_force = (
        backward_diff(padded[3], 0) + forward_diff(padded[1], 1) + backward_diff(padded[5], 2)
    )
    depth_force = (
        backward_diff(padded[4], 0) + backward_diff(padded[5], 1) + forward_diff(padded[2], 2)
    )
    return velocity + step_ratio * buoyancy * jnp.stack([strike_force, cross_force, depth_force])


def stress_update(stress, padded, lame, shear):
    stretch_strike = backward_diff(padded[0], 0)
    stretch_cross = backward_diff(padded[1], 1)
    stretch_depth = backward_diff(padded[2], 2)
    dilation = stretch_strike + stretch_cross + stretch_depth
    normal = jnp.stack(
        [
            lame * dilation + 2.0 * shear * stretch_strike,
            lame * dilation + 2.0 * shear * stretch_cross,
            lame * dilation + 2.0 * shear * stretch_depth,
        ]
    )
    tangent = shear * jnp.stack(
        [
            forward_diff(padded[0], 1) + forward_diff(padded[1], 0),
            forward_diff(padded[0], 2) + forward_diff(padded[2], 0),
            forward_diff(padded[1], 2) + forward_diff(padded[2], 1),
        ]
    )
    return stress + step_ratio * jnp.concatenate([normal, tangent], 0)


def friction(trial, damping, prestress, normal_stress, rate_a, state):
    total = trial + prestress
    width = 2.0 * ref_rate * jnp.exp(-state / rate_a)
    strength = rate_a * normal_stress
    scaled = inverse_sinh(total / (damping * width))
    for iteration in range(NEWTON):
        residual = strength * scaled + damping * width * jnp.sinh(scaled) - total
        slope = strength + damping * width * jnp.cosh(scaled)
        scaled = scaled - residual / slope
    slip = width * jnp.sinh(scaled)
    traction = total - damping * slip
    evolved = state + evolve_rate * (
        jnp.exp((base_friction - state) / evolve_b) - jnp.abs(slip) / ref_rate
    )
    return (traction - prestress, slip, evolved)


def pad_depth(field):
    return jnp.pad(field, ((0, 0), (0, 0), (0, 0), (2, 2)))


def local(
    velocity, stress, buoyancy, lame, shear, fault_tile, prestress, normal_stress, rate_a, state
):
    strike_pos = lax.axis_index("strike")
    cross_pos = lax.axis_index("cross")
    is_owner = fault_tile[strike_pos] == cross_pos
    damping = 0.5 * jnp.sqrt(shear[:, 0, :] / buoyancy[:, 0, :])
    fault_prestress, fault_normal, fault_rate, fault_state = (
        lax.all_gather(prestress, "cross", axis=1, tiled=True),
        lax.all_gather(normal_stress, "cross", axis=1, tiled=True),
        lax.all_gather(rate_a, "cross", axis=1, tiled=True),
        lax.all_gather(state, "cross", axis=1, tiled=True),
    )
    slip = jnp.zeros_like(fault_state)
    for iteration in range(STEPS):
        stress_wide = with_halo(stress, (("strike", 1), ("cross", 2)), 2)
        velocity = velocity_update(velocity, pad_depth(stress_wide), buoyancy)
        velocity_wide = with_halo(velocity, (("strike", 1), ("cross", 2)), 2)
        stress = stress_update(stress, pad_depth(velocity_wide), lame, shear)
        trial = stress[3, :, 0, :]
        change, slip, fault_state = friction(
            trial, damping, fault_prestress, fault_normal, fault_rate, fault_state
        )
        update = jnp.where(is_owner, change, trial)
        stress = stress.at[3, :, 0, :].set(update)
    slip_out, state_out = (
        lax.psum_scatter(jnp.where(is_owner, slip, 0.0), "cross", scatter_dimension=1, tiled=True),
        lax.psum_scatter(
            jnp.where(is_owner, fault_state, 0.0), "cross", scatter_dimension=1, tiled=True
        ),
    )
    return (velocity, stress, slip_out, state_out)


def solution(mesh):
    in_specs = (
        P(None, "strike", "cross", None),
        P(None, "strike", "cross", None),
        P("strike", "cross", None),
        P("strike", "cross", None),
        P("strike", "cross", None),
        P(),
        P("strike", "cross"),
        P("strike", "cross"),
        P("strike", "cross"),
        P("strike", "cross"),
    )
    out_specs = (
        P(None, "strike", "cross", None),
        P(None, "strike", "cross", None),
        P("strike", "cross"),
        P("strike", "cross"),
    )
    return jax.shard_map(local, mesh=mesh, in_specs=in_specs, out_specs=out_specs, check_vma=False)
```

profile of v0, /device:TPU:32, one launch (start us, length us, event | category | flops | bytes accessed | tf_op | source)
XLA Modules:
  0.0 468.4 jit_solution(657342428143192859)
XLA Ops:
  7.2 2.3 copy.51
  9.7 1.9 collective-permute-start
  11.6 6.0 %collective-permute-start.1 = (f32[6,2,16,256]{3,1,2,0:T(2,128)S(1)}, f32[6,2,16,256]{3,1,2,0:T(2,128)S(1)}, u32[]{:S(2)}, u32[]{:S(2)}) collective-permute-start(f32[6,2,16,256]{3,1,2,0:T(2,128)S(1)} %get-tuple-element.137), channel_id=1, source_target_pairs={{8,0},{16,8},{24,16},{32,24},{40,32},{48,40},{56,48},{64,56},{72,6... | collective-permute-start | bytes 589832 | tf_op jit(solution)/shard_map/ppermute | solution.py:25
  17.7 1.4 collective-permute-done
  19.1 1.8 collective-permute-done.1
  20.9 3.5 collective-permute-start.2
  24.5 1.3 collective-permute-start.3
  26.0 11.5 %collective-permute-done.2 = f32[6,20,2,256]{3,1,2,0:T(8,128)S(1)} collective-permute-done((f32[6,20,2,256]{3,1,2,0:T(8,128)S(1)}, f32[6,20,2,256]{3,1,2,0:T(8,128)S(1)}, u32[]{:S(2)}, u32[]{:S(2)}) %collective-permute-start.2) | collective-permute-done | bytes 245792 | tf_op jit(solution)/shard_map/ppermute | solution.py:24
  37.5 3.0 select_maximum_fusion.12
  44.1 2.7 collective-permute-start.4
  46.8 5.3 %collective-permute-start.5 = (f32[3,2,16,256]{3,1,2,0:T(2,128)S(1)}, f32[3,2,16,256]{3,1,2,0:T(2,128)S(1)}, u32[]{:S(2)}, u32[]{:S(2)}) collective-permute-start(f32[3,2,16,256]{3,1,2,0:T(2,128)S(1)} %get-tuple-element.157), channel_id=1, source_target_pairs={{8,0},{16,8},{24,16},{32,24},{40,32},{48,40},{56,48},{64,56},{72,6... | collective-permute-start | bytes 294920 | tf_op jit(solution)/shard_map/ppermute | solution.py:25
  52.5 1.8 collective-permute-done.5
  54.3 4.4 collective-permute-start.6
  58.7 1.3 collective-permute-start.7
  60.1 31.8 %all-gather = f32[8,32,16]{1,2,0:T(8,128)S(1)} all-gather(f32[1,32,16]{1,2,0:T(8,128)S(1)} %bitcast.312), channel_id=1, replica_groups=mesh['strike'=32,'cross'=8] {'cross'}, dimensions={0}, use_global_device_ids=true | all-gather | bytes 18432 | tf_op jit(solution)/shard_map/all_gather | solution.py:119
  92.0 28.2 %all-gather.3 = f32[8,32,16]{1,2,0:T(8,128)S(1)} all-gather(f32[1,32,16]{1,2,0:T(8,128)S(1)} %bitcast.313), channel_id=1, replica_groups=mesh['strike'=32,'cross'=8] {'cross'}, dimensions={0}, use_global_device_ids=true | all-gather | bytes 18432 | tf_op jit(solution)/shard_map/all_gather | solution.py:120
  120.2 28.2 %all-gather.2 = f32[8,32,16]{1,2,0:T(8,128)S(1)} all-gather(f32[1,32,16]{1,2,0:T(8,128)S(1)} %bitcast.314), channel_id=1, replica_groups=mesh['strike'=32,'cross'=8] {'cross'}, dimensions={0}, use_global_device_ids=true | all-gather | bytes 18432 | tf_op jit(solution)/shard_map/all_gather | solution.py:121
  148.5 28.3 %all-gather.1 = f32[8,32,16]{1,2,0:T(8,128)S(1)} all-gather(f32[1,32,16]{1,2,0:T(8,128)S(1)} %bitcast.315), channel_id=1, replica_groups=mesh['strike'=32,'cross'=8] {'cross'}, dimensions={0}, use_global_device_ids=true | all-gather | bytes 18432 | tf_op jit(solution)/shard_map/all_gather | solution.py:122
  185.6 1.9 collective-permute-start.8
  187.5 6.0 %collective-permute-start.9 = (f32[6,2,16,256]{3,1,2,0:T(2,128)S(1)}, f32[6,2,16,256]{3,1,2,0:T(2,128)S(1)}, u32[]{:S(2)}, u32[]{:S(2)}) collective-permute-start(f32[6,2,16,256]{3,1,2,0:T(2,128)S(1)} %get-tuple-element.135), channel_id=1, source_target_pairs={{8,0},{16,8},{24,16},{32,24},{40,32},{48,40},{56,48},{64,56},{72,6... | collective-permute-start | bytes 589832 | tf_op jit(solution)/shard_map/ppermute | solution.py:25
  193.6 1.4 collective-permute-done.8
  195.0 1.8 collective-permute-done.9
  196.9 1.3 collective-permute-start.10
  198.2 1.3 collective-permute-start.11
  199.5 12.4 %collective-permute-done.10 = f32[6,20,2,256]{3,1,2,0:T(8,128)S(1)} collective-permute-done((f32[6,20,2,256]{3,1,2,0:T(8,128)S(1)}, f32[6,20,2,256]{3,1,2,0:T(8,128)S(1)}, u32[]{:S(2)}, u32[]{:S(2)}) %collective-permute-start.10) | collective-permute-done | bytes 245792 | tf_op jit(solution)/shard_map/ppermute | solution.py:24
  211.9 3.0 select_maximum_fusion.8
  218.3 1.9 collective-permute-start.12
  220.3 6.0 %collective-permute-start.13 = (f32[3,2,16,256]{3,1,2,0:T(2,128)S(1)}, f32[3,2,16,256]{3,1,2,0:T(2,128)S(1)}, u32[]{:S(2)}, u32[]{:S(2)}) collective-permute-start(f32[3,2,16,256]{3,1,2,0:T(2,128)S(1)} %get-tuple-element.155), channel_id=1, source_target_pairs={{8,0},{16,8},{24,16},{32,24},{40,32},{48,40},{56,48},{64,56},{72,6... | collective-permute-start | bytes 294920 | tf_op jit(solution)/shard_map/ppermute | solution.py:25
  226.7 1.8 collective-permute-done.13
  228.6 4.4 collective-permute-start.14
  232.9 1.5 collective-permute-start.15
  235.6 4.4 collective-permute-done.15
  244.8 1.9 collective-permute-start.16
  246.7 6.0 %collective-permute-start.17 = (f32[6,2,16,256]{3,1,2,0:T(2,128)S(1)}, f32[6,2,16,256]{3,1,2,0:T(2,128)S(1)}, u32[]{:S(2)}, u32[]{:S(2)}) collective-permute-start(f32[6,2,16,256]{3,1,2,0:T(2,128)S(1)} %get-tuple-element.133), channel_id=1, source_target_pairs={{8,0},{16,8},{24,16},{32,24},{40,32},{48,40},{56,48},{64,56},{72,6... | collective-permute-start | bytes 589832 | tf_op jit(solution)/shard_map/ppermute | solution.py:25
  252.8 1.4 collective-permute-done.16
  254.2 1.8 collective-permute-done.17
  256.1 4.8 %collective-permute-start.18 = (f32[6,20,2,256]{3,1,2,0:T(8,128)S(1)}, f32[6,20,2,256]{3,1,2,0:T(8,128)S(1)}, u32[]{:S(2)}, u32[]{:S(2)}) collective-permute-start(f32[6,20,2,256]{3,1,2,0:T(8,128)S(1)} %get-tuple-element.124), channel_id=1, source_target_pairs={{0,1},{1,2},{2,3},{3,4},{4,5},{5,6},{6,7},{8,9},{9,10},{10,11},{11... | collective-permute-start | bytes 737288 | tf_op jit(solution)/shard_map/ppermute | solution.py:24
  262.2 11.6 %collective-permute-done.18 = f32[6,20,2,256]{3,1,2,0:T(8,128)S(1)} collective-permute-done((f32[6,20,2,256]{3,1,2,0:T(8,128)S(1)}, f32[6,20,2,256]{3,1,2,0:T(8,128)S(1)}, u32[]{:S(2)}, u32[]{:S(2)}) %collective-permute-start.18) | collective-permute-done | bytes 245792 | tf_op jit(solution)/shard_map/ppermute | solution.py:24
  273.7 3.0 select_maximum_fusion.4
  280.3 1.9 collective-permute-start.20
  282.3 6.0 %collective-permute-start.21 = (f32[3,2,16,256]{3,1,2,0:T(2,128)S(1)}, f32[3,2,16,256]{3,1,2,0:T(2,128)S(1)}, u32[]{:S(2)}, u32[]{:S(2)}) collective-permute-start(f32[3,2,16,256]{3,1,2,0:T(2,128)S(1)} %get-tuple-element.153), channel_id=1, source_target_pairs={{8,0},{16,8},{24,16},{32,24},{40,32},{48,40},{56,48},{64,56},{72,6... | collective-permute-start | bytes 294920 | tf_op jit(solution)/shard_map/ppermute | solution.py:25
  288.7 1.8 collective-permute-done.21
  290.6 4.4 collective-permute-start.22
  295.0 1.7 collective-permute-start.23
  297.6 4.4 collective-permute-done.23
  306.8 1.9 collective-permute-start.24
  308.7 6.0 %collective-permute-start.25 = (f32[6,2,16,256]{3,1,2,0:T(2,128)S(1)}, f32[6,2,16,256]{3,1,2,0:T(2,128)S(1)}, u32[]{:S(2)}, u32[]{:S(2)}) collective-permute-start(f32[6,2,16,256]{3,1,2,0:T(2,128)S(1)} %get-tuple-element.131), channel_id=1, source_target_pairs={{8,0},{16,8},{24,16},{32,24},{40,32},{48,40},{56,48},{64,56},{72,6... | collective-permute-start | bytes 589832 | tf_op jit(solution)/shard_map/ppermute | solution.py:25
  314.8 1.4 collective-permute-done.24
  316.2 1.8 collective-permute-done.25
  318.1 4.8 %collective-permute-start.26 = (f32[6,20,2,256]{3,1,2,0:T(8,128)S(1)}, f32[6,20,2,256]{3,1,2,0:T(8,128)S(1)}, u32[]{:S(2)}, u32[]{:S(2)}) collective-permute-start(f32[6,20,2,256]{3,1,2,0:T(8,128)S(1)} %get-tuple-element.122), channel_id=1, source_target_pairs={{0,1},{1,2},{2,3},{3,4},{4,5},{5,6},{6,7},{8,9},{9,10},{10,11},{11... | collective-permute-start | bytes 737288 | tf_op jit(solution)/shard_map/ppermute | solution.py:24
  324.2 11.6 %collective-permute-done.26 = f32[6,20,2,256]{3,1,2,0:T(8,128)S(1)} collective-permute-done((f32[6,20,2,256]{3,1,2,0:T(8,128)S(1)}, f32[6,20,2,256]{3,1,2,0:T(8,128)S(1)}, u32[]{:S(2)}, u32[]{:S(2)}) %collective-permute-start.26) | collective-permute-done | bytes 245792 | tf_op jit(solution)/shard_map/ppermute | solution.py:24
  335.8 3.0 select_maximum_fusion
  342.4 1.9 collective-permute-start.28
  344.3 6.0 %collective-permute-start.29 = (f32[3,2,16,256]{3,1,2,0:T(2,128)S(1)}, f32[3,2,16,256]{3,1,2,0:T(2,128)S(1)}, u32[]{:S(2)}, u32[]{:S(2)}) collective-permute-start(f32[3,2,16,256]{3,1,2,0:T(2,128)S(1)} %get-tuple-element.151), channel_id=1, source_target_pairs={{8,0},{16,8},{24,16},{32,24},{40,32},{48,40},{56,48},{64,56},{72,6... | collective-permute-start | bytes 294920 | tf_op jit(solution)/shard_map/ppermute | solution.py:25
  350.8 1.8 collective-permute-done.29
  352.6 4.4 collective-permute-start.30
  357.0 1.5 collective-permute-start.31
  358.5 1.3 copy.68
  359.8 4.2 collective-permute-done.31
  370.3 2.0 copy.69
  372.4 46.8 %reduce-scatter.7.cloned.1.call-done = f32[32,16]{1,0:T(8,128)} async-done(((f32[256,16]{1,0:T(8,128)}), f32[32,16]{1,0:T(8,128)}) %reduce-scatter.7.cloned.1.call-update) | async-done | bytes 2064
  419.2 1.4 copy.71
  420.6 39.4 %reduce-scatter.9.cloned.1.call-done = f32[32,16]{1,0:T(8,128)} async-done(((f32[256,16]{1,0:T(8,128)}), f32[32,16]{1,0:T(8,128)}) %reduce-scatter.9.cloned.1.call-update) | async-done | bytes 2064
  460.0 1.4 copy.73
  (132 shorter events, 45.4 us)
Async XLA Ops:
  7.2 412.0 %reduce-scatter.7.cloned.1.call-start = ((), (), s32[]{:S(2)}) async-start(), calls=%async_computation.2 | async-start | bytes 147456
  9.5 16.2 %copy-start.4 = (f32[16,16,256]{2,1,0:T(8,128)S(1)}, f32[16,16,256]{2,1,0:T(8,128)}, u32[]{:S(2)}) copy-start(f32[16,16,256]{2,1,0:T(8,128)} %param.20) | copy-start | bytes 786436
  9.7 9.4 %collective-permute-start = (f32[6,2,16,256]{3,1,2,0:T(2,128)S(1)}, f32[6,2,16,256]{3,1,2,0:T(2,128)S(1)}, u32[]{:S(2)}, u32[]{:S(2)}) collective-permute-start(f32[6,2,16,256]{3,1,2,0:T(2,128)S(1)} %get-tuple-element.136), channel_id=1, source_target_pairs={{0,8},{8,16},{16,24},{24,32},{32,40},{40,48},{48,56},{56,64},{64,7... | collective-permute-start | bytes 589832 | tf_op jit(solution)/shard_map/ppermute | solution.py:24
  11.6 9.2 %collective-permute-start.1 = (f32[6,2,16,256]{3,1,2,0:T(2,128)S(1)}, f32[6,2,16,256]{3,1,2,0:T(2,128)S(1)}, u32[]{:S(2)}, u32[]{:S(2)}) collective-permute-start(f32[6,2,16,256]{3,1,2,0:T(2,128)S(1)} %get-tuple-element.137), channel_id=1, source_target_pairs={{8,0},{16,8},{24,16},{32,24},{40,32},{48,40},{56,48},{64,56},{72,6... | collective-permute-start | bytes 589832 | tf_op jit(solution)/shard_map/ppermute | solution.py:25
  20.9 16.5 %collective-permute-start.2 = (f32[6,20,2,256]{3,1,2,0:T(8,128)S(1)}, f32[6,20,2,256]{3,1,2,0:T(8,128)S(1)}, u32[]{:S(2)}, u32[]{:S(2)}) collective-permute-start(f32[6,20,2,256]{3,1,2,0:T(8,128)S(1)} %get-tuple-element.128), channel_id=1, source_target_pairs={{0,1},{1,2},{2,3},{3,4},{4,5},{5,6},{6,7},{8,9},{9,10},{10,11},{11... | collective-permute-start | bytes 737288 | tf_op jit(solution)/shard_map/ppermute | solution.py:24
  24.5 13.0 %collective-permute-start.3 = (f32[6,20,2,256]{3,1,2,0:T(8,128)S(1)}, f32[6,20,2,256]{3,1,2,0:T(8,128)S(1)}, u32[]{:S(2)}, u32[]{:S(2)}) collective-permute-start(f32[6,20,2,256]{3,1,2,0:T(8,128)S(1)} %get-tuple-element.129), channel_id=1, source_target_pairs={{1,0},{2,1},{3,2},{4,3},{5,4},{6,5},{7,6},{9,8},{10,9},{11,10},{12... | collective-permute-start | bytes 737288 | tf_op jit(solution)/shard_map/ppermute | solution.py:25
  42.4 1.1 copy-start.1
  43.5 16.6 %copy-start.5 = (f32[16,32]{1,0:T(8,128)S(1)}, f32[16,32]{1,0:T(8,128)}, u32[]{:S(2)}) copy-start(f32[16,32]{1,0:T(8,128)} %param.24) | copy-start | bytes 6148
  43.5 48.4 %copy-start.6 = (f32[16,32]{1,0:T(8,128)S(1)}, f32[16,32]{1,0:T(8,128)}, u32[]{:S(2)}) copy-start(f32[16,32]{1,0:T(8,128)} %param.25) | copy-start | bytes 6148
  43.5 76.7 %copy-start.7 = (f32[16,32]{1,0:T(8,128)S(1)}, f32[16,32]{1,0:T(8,128)}, u32[]{:S(2)}) copy-start(f32[16,32]{1,0:T(8,128)} %param.26) | copy-start | bytes 6148
  43.5 105.0 %copy-start.8 = (f32[16,32]{1,0:T(8,128)S(1)}, f32[16,32]{1,0:T(8,128)}, u32[]{:S(2)}) copy-start(f32[16,32]{1,0:T(8,128)} %param.27) | copy-start | bytes 6148
  44.1 8.3 %collective-permute-start.4 = (f32[3,2,16,256]{3,1,2,0:T(2,128)S(1)}, f32[3,2,16,256]{3,1,2,0:T(2,128)S(1)}, u32[]{:S(2)}, u32[]{:S(2)}) collective-permute-start(f32[3,2,16,256]{3,1,2,0:T(2,128)S(1)} %get-tuple-element.156), channel_id=1, source_target_pairs={{0,8},{8,16},{16,24},{24,32},{32,40},{40,48},{48,56},{56,64},{64,7... | collective-permute-start | bytes 294920 | tf_op jit(solution)/shard_map/ppermute | solution.py:24
  46.8 7.5 %collective-permute-start.5 = (f32[3,2,16,256]{3,1,2,0:T(2,128)S(1)}, f32[3,2,16,256]{3,1,2,0:T(2,128)S(1)}, u32[]{:S(2)}, u32[]{:S(2)}) collective-permute-start(f32[3,2,16,256]{3,1,2,0:T(2,128)S(1)} %get-tuple-element.157), channel_id=1, source_target_pairs={{8,0},{16,8},{24,16},{32,24},{40,32},{48,40},{56,48},{64,56},{72,6... | collective-permute-start | bytes 294920 | tf_op jit(solution)/shard_map/ppermute | solution.py:25
  54.3 124.5 %collective-permute-start.6 = (f32[3,20,2,256]{3,1,2,0:T(8,128)S(1)}, f32[3,20,2,256]{3,1,2,0:T(8,128)S(1)}, u32[]{:S(2)}, u32[]{:S(2)}) collective-permute-start(f32[3,20,2,256]{3,1,2,0:T(8,128)S(1)} %get-tuple-element.148), channel_id=1, source_target_pairs={{0,1},{1,2},{2,3},{3,4},{4,5},{5,6},{6,7},{8,9},{9,10},{10,11},{11... | collective-permute-start | bytes 368648 | tf_op jit(solution)/shard_map/ppermute | solution.py:24
  58.7 120.1 %collective-permute-start.7 = (f32[3,20,2,256]{3,1,2,0:T(8,128)S(1)}, f32[3,20,2,256]{3,1,2,0:T(8,128)S(1)}, u32[]{:S(2)}, u32[]{:S(2)}) collective-permute-start(f32[3,20,2,256]{3,1,2,0:T(8,128)S(1)} %get-tuple-element.149), channel_id=1, source_target_pairs={{1,0},{2,1},{3,2},{4,3},{5,4},{6,5},{7,6},{9,8},{10,9},{11,10},{12... | collective-permute-start | bytes 368648 | tf_op jit(solution)/shard_map/ppermute | solution.py:25
  180.7 1.0 copy-start
  180.7 1.0 copy-start.3
  182.7 1.4 copy-start.2
  185.6 9.4 %collective-permute-start.8 = (f32[6,2,16,256]{3,1,2,0:T(2,128)S(1)}, f32[6,2,16,256]{3,1,2,0:T(2,128)S(1)}, u32[]{:S(2)}, u32[]{:S(2)}) collective-permute-start(f32[6,2,16,256]{3,1,2,0:T(2,128)S(1)} %get-tuple-element.134), channel_id=1, source_target_pairs={{0,8},{8,16},{16,24},{24,32},{32,40},{40,48},{48,56},{56,64},{64,7... | collective-permute-start | bytes 589832 | tf_op jit(solution)/shard_map/ppermute | solution.py:24
  187.5 9.3 %collective-permute-start.9 = (f32[6,2,16,256]{3,1,2,0:T(2,128)S(1)}, f32[6,2,16,256]{3,1,2,0:T(2,128)S(1)}, u32[]{:S(2)}, u32[]{:S(2)}) collective-permute-start(f32[6,2,16,256]{3,1,2,0:T(2,128)S(1)} %get-tuple-element.135), channel_id=1, source_target_pairs={{8,0},{16,8},{24,16},{32,24},{40,32},{48,40},{56,48},{64,56},{72,6... | collective-permute-start | bytes 589832 | tf_op jit(solution)/shard_map/ppermute | solution.py:25
  196.9 15.0 %collective-permute-start.10 = (f32[6,20,2,256]{3,1,2,0:T(8,128)S(1)}, f32[6,20,2,256]{3,1,2,0:T(8,128)S(1)}, u32[]{:S(2)}, u32[]{:S(2)}) collective-permute-start(f32[6,20,2,256]{3,1,2,0:T(8,128)S(1)} %get-tuple-element.126), channel_id=1, source_target_pairs={{0,1},{1,2},{2,3},{3,4},{4,5},{5,6},{6,7},{8,9},{9,10},{10,11},{11... | collective-permute-start | bytes 737288 | tf_op jit(solution)/shard_map/ppermute | solution.py:24
  198.2 13.7 %collective-permute-start.11 = (f32[6,20,2,256]{3,1,2,0:T(8,128)S(1)}, f32[6,20,2,256]{3,1,2,0:T(8,128)S(1)}, u32[]{:S(2)}, u32[]{:S(2)}) collective-permute-start(f32[6,20,2,256]{3,1,2,0:T(8,128)S(1)} %get-tuple-element.127), channel_id=1, source_target_pairs={{1,0},{2,1},{3,2},{4,3},{5,4},{6,5},{7,6},{9,8},{10,9},{11,10},{12... | collective-permute-start | bytes 737288 | tf_op jit(solution)/shard_map/ppermute | solution.py:25
  218.3 8.3 %collective-permute-start.12 = (f32[3,2,16,256]{3,1,2,0:T(2,128)S(1)}, f32[3,2,16,256]{3,1,2,0:T(2,128)S(1)}, u32[]{:S(2)}, u32[]{:S(2)}) collective-permute-start(f32[3,2,16,256]{3,1,2,0:T(2,128)S(1)} %get-tuple-element.154), channel_id=1, source_target_pairs={{0,8},{8,16},{16,24},{24,32},{32,40},{40,48},{48,56},{56,64},{64,7... | collective-permute-start | bytes 294920 | tf_op jit(solution)/shard_map/ppermute | solution.py:24
  220.3 8.2 %collective-permute-start.13 = (f32[3,2,16,256]{3,1,2,0:T(2,128)S(1)}, f32[3,2,16,256]{3,1,2,0:T(2,128)S(1)}, u32[]{:S(2)}, u32[]{:S(2)}) collective-permute-start(f32[3,2,16,256]{3,1,2,0:T(2,128)S(1)} %get-tuple-element.155), channel_id=1, source_target_pairs={{8,0},{16,8},{24,16},{32,24},{40,32},{48,40},{56,48},{64,56},{72,6... | collective-permute-start | bytes 294920 | tf_op jit(solution)/shard_map/ppermute | solution.py:25
  228.6 7.0 %collective-permute-start.14 = (f32[3,20,2,256]{3,1,2,0:T(8,128)S(1)}, f32[3,20,2,256]{3,1,2,0:T(8,128)S(1)}, u32[]{:S(2)}, u32[]{:S(2)}) collective-permute-start(f32[3,20,2,256]{3,1,2,0:T(8,128)S(1)} %get-tuple-element.146), channel_id=1, source_target_pairs={{0,1},{1,2},{2,3},{3,4},{4,5},{5,6},{6,7},{8,9},{9,10},{10,11},{11... | collective-permute-start | bytes 368648 | tf_op jit(solution)/shard_map/ppermute | solution.py:24
  232.9 7.1 %collective-permute-start.15 = (f32[3,20,2,256]{3,1,2,0:T(8,128)S(1)}, f32[3,20,2,256]{3,1,2,0:T(8,128)S(1)}, u32[]{:S(2)}, u32[]{:S(2)}) collective-permute-start(f32[3,20,2,256]{3,1,2,0:T(8,128)S(1)} %get-tuple-element.147), channel_id=1, source_target_pairs={{1,0},{2,1},{3,2},{4,3},{5,4},{6,5},{7,6},{9,8},{10,9},{11,10},{12... | collective-permute-start | bytes 368648 | tf_op jit(solution)/shard_map/ppermute | solution.py:25
  244.8 9.4 %collective-permute-start.16 = (f32[6,2,16,256]{3,1,2,0:T(2,128)S(1)}, f32[6,2,16,256]{3,1,2,0:T(2,128)S(1)}, u32[]{:S(2)}, u32[]{:S(2)}) collective-permute-start(f32[6,2,16,256]{3,1,2,0:T(2,128)S(1)} %get-tuple-element.132), channel_id=1, source_target_pairs={{0,8},{8,16},{16,24},{24,32},{32,40},{40,48},{48,56},{56,64},{64,7... | collective-permute-start | bytes 589832 | tf_op jit(solution)/shard_map/ppermute | solution.py:24
  246.7 9.3 %collective-permute-start.17 = (f32[6,2,16,256]{3,1,2,0:T(2,128)S(1)}, f32[6,2,16,256]{3,1,2,0:T(2,128)S(1)}, u32[]{:S(2)}, u32[]{:S(2)}) collective-permute-start(f32[6,2,16,256]{3,1,2,0:T(2,128)S(1)} %get-tuple-element.133), channel_id=1, source_target_pairs={{8,0},{16,8},{24,16},{32,24},{40,32},{48,40},{56,48},{64,56},{72,6... | collective-permute-start | bytes 589832 | tf_op jit(solution)/shard_map/ppermute | solution.py:25
  256.1 17.7 %collective-permute-start.18 = (f32[6,20,2,256]{3,1,2,0:T(8,128)S(1)}, f32[6,20,2,256]{3,1,2,0:T(8,128)S(1)}, u32[]{:S(2)}, u32[]{:S(2)}) collective-permute-start(f32[6,20,2,256]{3,1,2,0:T(8,128)S(1)} %get-tuple-element.124), channel_id=1, source_target_pairs={{0,1},{1,2},{2,3},{3,4},{4,5},{5,6},{6,7},{8,9},{9,10},{10,11},{11... | collective-permute-start | bytes 737288 | tf_op jit(solution)/shard_map/ppermute | solution.py:24
  260.9 12.9 %collective-permute-start.19 = (f32[6,20,2,256]{3,1,2,0:T(8,128)S(1)}, f32[6,20,2,256]{3,1,2,0:T(8,128)S(1)}, u32[]{:S(2)}, u32[]{:S(2)}) collective-permute-start(f32[6,20,2,256]{3,1,2,0:T(8,128)S(1)} %get-tuple-element.125), channel_id=1, source_target_pairs={{1,0},{2,1},{3,2},{4,3},{5,4},{6,5},{7,6},{9,8},{10,9},{11,10},{12... | collective-permute-start | bytes 737288 | tf_op jit(solution)/shard_map/ppermute | solution.py:25
  280.3 8.4 %collective-permute-start.20 = (f32[3,2,16,256]{3,1,2,0:T(2,128)S(1)}, f32[3,2,16,256]{3,1,2,0:T(2,128)S(1)}, u32[]{:S(2)}, u32[]{:S(2)}) collective-permute-start(f32[3,2,16,256]{3,1,2,0:T(2,128)S(1)} %get-tuple-element.152), channel_id=1, source_target_pairs={{0,8},{8,16},{16,24},{24,32},{32,40},{40,48},{48,56},{56,64},{64,7... | collective-permute-start | bytes 294920 | tf_op jit(solution)/shard_map/ppermute | solution.py:24
  282.3 8.2 %collective-permute-start.21 = (f32[3,2,16,256]{3,1,2,0:T(2,128)S(1)}, f32[3,2,16,256]{3,1,2,0:T(2,128)S(1)}, u32[]{:S(2)}, u32[]{:S(2)}) collective-permute-start(f32[3,2,16,256]{3,1,2,0:T(2,128)S(1)} %get-tuple-element.153), channel_id=1, source_target_pairs={{8,0},{16,8},{24,16},{32,24},{40,32},{48,40},{56,48},{64,56},{72,6... | collective-permute-start | bytes 294920 | tf_op jit(solution)/shard_map/ppermute | solution.py:25
  290.6 7.1 %collective-permute-start.22 = (f32[3,20,2,256]{3,1,2,0:T(8,128)S(1)}, f32[3,20,2,256]{3,1,2,0:T(8,128)S(1)}, u32[]{:S(2)}, u32[]{:S(2)}) collective-permute-start(f32[3,20,2,256]{3,1,2,0:T(8,128)S(1)} %get-tuple-element.144), channel_id=1, source_target_pairs={{0,1},{1,2},{2,3},{3,4},{4,5},{5,6},{6,7},{8,9},{9,10},{10,11},{11... | collective-permute-start | bytes 368648 | tf_op jit(solution)/shard_map/ppermute | solution.py:24
  295.0 7.0 %collective-permute-start.23 = (f32[3,20,2,256]{3,1,2,0:T(8,128)S(1)}, f32[3,20,2,256]{3,1,2,0:T(8,128)S(1)}, u32[]{:S(2)}, u32[]{:S(2)}) collective-permute-start(f32[3,20,2,256]{3,1,2,0:T(8,128)S(1)} %get-tuple-element.145), channel_id=1, source_target_pairs={{1,0},{2,1},{3,2},{4,3},{5,4},{6,5},{7,6},{9,8},{10,9},{11,10},{12... | collective-permute-start | bytes 368648 | tf_op jit(solution)/shard_map/ppermute | solution.py:25
  306.8 9.4 %collective-permute-start.24 = (f32[6,2,16,256]{3,1,2,0:T(2,128)S(1)}, f32[6,2,16,256]{3,1,2,0:T(2,128)S(1)}, u32[]{:S(2)}, u32[]{:S(2)}) collective-permute-start(f32[6,2,16,256]{3,1,2,0:T(2,128)S(1)} %get-tuple-element.130), channel_id=1, source_target_pairs={{0,8},{8,16},{16,24},{24,32},{32,40},{40,48},{48,56},{56,64},{64,7... | collective-permute-start | bytes 589832 | tf_op jit(solution)/shard_map/ppermute | solution.py:24
  308.7 9.3 %collective-permute-start.25 = (f32[6,2,16,256]{3,1,2,0:T(2,128)S(1)}, f32[6,2,16,256]{3,1,2,0:T(2,128)S(1)}, u32[]{:S(2)}, u32[]{:S(2)}) collective-permute-start(f32[6,2,16,256]{3,1,2,0:T(2,128)S(1)} %get-tuple-element.131), channel_id=1, source_target_pairs={{8,0},{16,8},{24,16},{32,24},{40,32},{48,40},{56,48},{64,56},{72,6... | collective-permute-start | bytes 589832 | tf_op jit(solution)/shard_map/ppermute | solution.py:25
  318.1 17.7 %collective-permute-start.26 = (f32[6,20,2,256]{3,1,2,0:T(8,128)S(1)}, f32[6,20,2,256]{3,1,2,0:T(8,128)S(1)}, u32[]{:S(2)}, u32[]{:S(2)}) collective-permute-start(f32[6,20,2,256]{3,1,2,0:T(8,128)S(1)} %get-tuple-element.122), channel_id=1, source_target_pairs={{0,1},{1,2},{2,3},{3,4},{4,5},{5,6},{6,7},{8,9},{9,10},{10,11},{11... | collective-permute-start | bytes 737288 | tf_op jit(solution)/shard_map/ppermute | solution.py:24
  322.9 12.9 %collective-permute-start.27 = (f32[6,20,2,256]{3,1,2,0:T(8,128)S(1)}, f32[6,20,2,256]{3,1,2,0:T(8,128)S(1)}, u32[]{:S(2)}, u32[]{:S(2)}) collective-permute-start(f32[6,20,2,256]{3,1,2,0:T(8,128)S(1)} %get-tuple-element.123), channel_id=1, source_target_pairs={{1,0},{2,1},{3,2},{4,3},{5,4},{6,5},{7,6},{9,8},{10,9},{11,10},{12... | collective-permute-start | bytes 737288 | tf_op jit(solution)/shard_map/ppermute | solution.py:25
  342.4 8.4 %collective-permute-start.28 = (f32[3,2,16,256]{3,1,2,0:T(2,128)S(1)}, f32[3,2,16,256]{3,1,2,0:T(2,128)S(1)}, u32[]{:S(2)}, u32[]{:S(2)}) collective-permute-start(f32[3,2,16,256]{3,1,2,0:T(2,128)S(1)} %get-tuple-element.150), channel_id=1, source_target_pairs={{0,8},{8,16},{16,24},{24,32},{32,40},{40,48},{48,56},{56,64},{64,7... | collective-permute-start | bytes 294920 | tf_op jit(solution)/shard_map/ppermute | solution.py:24
  344.3 8.2 %collective-permute-start.29 = (f32[3,2,16,256]{3,1,2,0:T(2,128)S(1)}, f32[3,2,16,256]{3,1,2,0:T(2,128)S(1)}, u32[]{:S(2)}, u32[]{:S(2)}) collective-permute-start(f32[3,2,16,256]{3,1,2,0:T(2,128)S(1)} %get-tuple-element.151), channel_id=1, source_target_pairs={{8,0},{16,8},{24,16},{32,24},{40,32},{48,40},{56,48},{64,56},{72,6... | collective-permute-start | bytes 294920 | tf_op jit(solution)/shard_map/ppermute | solution.py:25
  352.6 7.2 %collective-permute-start.30 = (f32[3,20,2,256]{3,1,2,0:T(8,128)S(1)}, f32[3,20,2,256]{3,1,2,0:T(8,128)S(1)}, u32[]{:S(2)}, u32[]{:S(2)}) collective-permute-start(f32[3,20,2,256]{3,1,2,0:T(8,128)S(1)} %get-tuple-element.142), channel_id=1, source_target_pairs={{0,1},{1,2},{2,3},{3,4},{4,5},{5,6},{6,7},{8,9},{9,10},{10,11},{11... | collective-permute-start | bytes 368648 | tf_op jit(solution)/shard_map/ppermute | solution.py:24
  357.0 7.0 %collective-permute-start.31 = (f32[3,20,2,256]{3,1,2,0:T(8,128)S(1)}, f32[3,20,2,256]{3,1,2,0:T(8,128)S(1)}, u32[]{:S(2)}, u32[]{:S(2)}) collective-permute-start(f32[3,20,2,256]{3,1,2,0:T(8,128)S(1)} %get-tuple-element.143), channel_id=1, source_target_pairs={{1,0},{2,1},{3,2},{4,3},{5,4},{6,5},{7,6},{9,8},{10,9},{11,10},{12... | collective-permute-start | bytes 368648 | tf_op jit(solution)/shard_map/ppermute | solution.py:25
  369.5 90.5 %reduce-scatter.9.cloned.1.call-start = ((), (), s32[]{:S(2)}) async-start(), calls=%async_computation.3 | async-start | bytes 147456
Sparse Core Ops, SparseCore 0:
  369.6 49.5 reduce-scatter.6
  421.9 38.0 reduce-scatter.8
where the time goes:
time: 475 us; the launch traced here: 468 us
  waiting for transfers between devices  170 us (36%)
  blocking collectives  116 us (24%)
  starting transfers between devices  107 us (23%)
  other arithmetic  43.4 us (9%)
  local copies, waits for them, and re-layouts  16 us (3%)
  between operations  15.8 us (3%)
    unnamed x4, waiting for transfers between devices  86.3 us
    ppermute x16, starting transfers between devices, with_halo(): after = lax.ppermute(first, axis, down)  58.7 us
    ppermute x16, waiting for transfers between devices, with_halo(): before = lax.ppermute(last, axis, up)  56.3 us
    ppermute x16, starting transfers between devices, with_halo(): before = lax.ppermute(last, axis, up)  48.1 us
    all_gather x1, blocking collectives, local(): lax.all_gather(prestress, 'cross', axis=1, tiled=True)  31.8 us
    all_gather x1, blocking collectives, local(): lax.all_gather(state, 'cross', axis=1, tiled=True)  28.3 us
    all_gather x1, blocking collectives, local(): lax.all_gather(normal_stress, 'cross', axis=1, tiled=True)  28.2 us
    all_gather x1, blocking collectives, local(): lax.all_gather(rate_a, 'cross', axis=1, tiled=True)  28.2 us
  transfers between devices with their start and end apart: 34, of which 27 were waited for; matrix products, arithmetic and copies ran while one was open for 2% of the time, Pallas kernels for 0%

commit v1 on v0

v1 whole, which is shorter than its diff:
```python
import jax
import jax.numpy as jnp
from jax import lax
from jax.experimental import pallas as pl
from jax.experimental.pallas import tpu as pltpu
from jax.sharding import PartitionSpec as P

STEPS = 4
NEWTON = 8

step_ratio = 0.25
ref_rate = 0.001
evolve_rate = 1e-05
base_friction = 0.6
evolve_b = 0.03

CX = 16
CY = 16
NZ = 256
MESH = pl.DeviceIdType.MESH

XX, XZ, XY, YZ, YY, ZZ = range(6)
STRESS_ORDER = (0, 4, 3, 5, 1, 2)
VX, VZ, VY = range(3)
VELOCITY_ORDER = (0, 2, 1)

NEAR = step_ratio * 1.125
FAR = step_ratio / 24.0

RUNS = ((0, 4), (12, 4), (4, 8))


def wave_kernel(
    stress_in,
    velocity_in,
    buoyancy_in,
    lame_in,
    shear_in,
    fault_tile,
    prestress,
    normal_stress,
    rate_a,
    state,
    velocity_out,
    stress_out,
    slip_out,
    state_out,
    stress,
    velocity,
    stress_halo,
    velocity_halo,
    buoyancy,
    lame,
    shear,
    trial,
    ratio,
    fault,
    packed,
    result,
    send_sem,
    recv_sem,
    pack_send,
    pack_recv,
    result_send,
    result_recv,
    load_sem,
    store_sem,
):
    strike = lax.axis_index("strike")
    cross = lax.axis_index("cross")
    n_strike = lax.axis_size("strike")
    n_cross = lax.axis_size("cross")
    has = {
        "up": strike + 1 < n_strike,
        "down": strike >= 1,
        "right": cross + 1 < n_cross,
        "left": cross >= 1,
    }
    place = {
        "up": (strike + 1, cross),
        "down": (strike - 1, cross),
        "right": (strike, cross + 1),
        "left": (strike, cross - 1),
    }
    opposite = {"up": "down", "down": "up", "right": "left", "left": "right"}

    loads = []
    for index, comp in enumerate(STRESS_ORDER):
        loads.append((stress_in.at[comp], stress.at[index, pl.ds(2, CX)]))
    loads.append((buoyancy_in, buoyancy))
    for index, comp in enumerate(VELOCITY_ORDER):
        loads.append((velocity_in.at[comp], velocity.at[index, pl.ds(2, CX)]))
    loads.append((lame_in, lame))
    loads.append((shear_in, shear))
    loads = [
        pltpu.make_async_copy(source, target, load_sem.at[index])
        for index, (source, target) in enumerate(loads)
    ]
    for copy in loads:
        copy.start()

    zero_slab = jnp.zeros((CY, NZ), jnp.float32)
    for index in range(3):
        for slab in (0, 1, 18, 19):
            stress[index, slab] = zero_slab
            velocity[index, slab] = zero_slab

    def clear(slab, carry):
        for index in range(3):
            stress_halo[index, slab] = zero_slab
            velocity_halo[index, slab] = zero_slab
        return carry

    lax.fori_loop(0, CX, clear, 0)

    for index, ref in enumerate((prestress, normal_stress, rate_a, state)):
        value = ref[...]
        columns = pl.ds(32 * index, 32)
        packed[cross, 0:4, columns] = value[0:4]
        packed[cross, 4:8, columns] = value[12:16]
        packed[cross, 8:16, columns] = value[4:12]

    barrier = pltpu.get_barrier_semaphore()
    for side in ("up", "down"):

        @pl.when(has[side])
        def _(side=side):
            pl.semaphore_signal(barrier, inc=1, device_id=place[side], device_id_type=MESH)

    for step in range(1, 8):
        other = lax.rem(cross + step, n_cross)
        pl.semaphore_signal(barrier, inc=1, device_id=(strike, other), device_id_type=MESH)
    pl.semaphore_wait(
        barrier, 7 + has["up"].astype(jnp.int32) + has["down"].astype(jnp.int32)
    )

    def remote(phase, index, side, source, target):
        return (
            side,
            pltpu.make_async_remote_copy(
                src_ref=source,
                dst_ref=target,
                send_sem=send_sem.at[phase, index],
                recv_sem=recv_sem.at[phase, index],
                device_id=place[side],
                device_id_type=MESH,
            ),
        )

    def stress_strike():
        return [
            remote(0, 0, "up", stress.at[1:3, 16:18], stress.at[1:3, 0:2]),
            remote(0, 1, "up", stress.at[0:1, 17:18], stress.at[0:1, 1:2]),
            remote(0, 2, "down", stress.at[1:3, 2:3], stress.at[1:3, 18:19]),
            remote(0, 3, "down", stress.at[0:1, 2:4], stress.at[0:1, 18:20]),
        ]

    def velocity_strike():
        return [
            remote(1, 0, "up", velocity.at[0:1, 16:18], velocity.at[0:1, 0:2]),
            remote(1, 1, "up", velocity.at[1:3, 17:18], velocity.at[1:3, 1:2]),
            remote(1, 2, "down", velocity.at[0:1, 2:3], velocity.at[0:1, 18:19]),
            remote(1, 3, "down", velocity.at[1:3, 2:4], velocity.at[1:3, 18:20]),
        ]

    def stress_cross(run):
        first, count = RUNS[run]
        own, halo = pl.ds(2 + first, count), pl.ds(first, count)
        base = 4 + 4 * run
        return [
            remote(
                0, base, "right", stress.at[2:4, own, 14:16], stress_halo.at[0:2, halo, 14:16]
            ),
            remote(
                0, base + 1, "right", stress.at[4:5, own, 15:16], stress_halo.at[2:3, halo, 15:16]
            ),
            remote(
                0, base + 2, "left", stress.at[2:4, own, 0:1], stress_halo.at[0:2, halo, 0:1]
            ),
            remote(
                0, base + 3, "left", stress.at[4:5, own, 0:2], stress_halo.at[2:3, halo, 0:2]
            ),
        ]

    def velocity_cross(run):
        first, count = RUNS[run]
        own, halo = pl.ds(2 + first, count), pl.ds(first, count)
        base = 4 + 4 * run
        return [
            remote(
                1, base, "right", velocity.at[2:3, own, 14:16], velocity_halo.at[2:3, halo, 14:16]
            ),
            remote(
                1,
                base + 1,
                "right",
                velocity.at[0:2, own, 15:16],
                velocity_halo.at[0:2, halo, 15:16],
            ),
            remote(
                1, base + 2, "left", velocity.at[2:3, own, 0:1], velocity_halo.at[2:3, halo, 0:1]
            ),
            remote(
                1, base + 3, "left", velocity.at[0:2, own, 0:2], velocity_halo.at[0:2, halo, 0:2]
            ),
        ]

    def start(copies):
        for side, copy in copies:

            @pl.when(has[side])
            def _(copy=copy):
                copy.start()

    def wait_recv(copies):
        for side, copy in copies:

            @pl.when(has[opposite[side]])
            def _(copy=copy):
                copy.wait_recv()

    def wait_send(copies):
        for side, copy in copies:

            @pl.when(has[side])
            def _(copy=copy):
                copy.wait_send()

    for copy in loads[:6]:
        copy.wait()
    start(stress_strike() + stress_cross(0) + stress_cross(1) + stress_cross(2))

    def pack_copy(step):
        other = lax.rem(cross + step, n_cross)
        return pltpu.make_async_remote_copy(
            src_ref=packed.at[cross],
            dst_ref=packed.at[cross],
            send_sem=pack_send.at[step],
            recv_sem=pack_recv.at[step],
            device_id=(strike, other),
            device_id_type=MESH,
        )

    for step in range(1, 8):
        pack_copy(step).start()

    for copy in loads[6:]:
        copy.wait()

    row = lax.broadcasted_iota(jnp.int32, (CY, NZ), 0)
    lane = lax.broadcasted_iota(jnp.int32, (CY, NZ), 1)

    def depth(value, offset):
        moved = pltpu.roll(value, (-offset) % NZ, 1)
        if offset < 0:
            return jnp.where(lane < -offset, 0.0, moved)
        return jnp.where(lane >= NZ - offset, 0.0, moved)

    def across(value, halo, offset):
        if offset < 0:
            joined = jnp.where(row >= CY + offset, halo, value)
        else:
            joined = jnp.where(row < offset, halo, value)
        return pltpu.roll(joined, (-offset) % CY, 0)

    def forward_depth(value):
        return (
            depth(value, 1) - value,
            depth(value, 2) - depth(value, -1),
        )

    def backward_depth(value):
        return (
            value - depth(value, -1),
            depth(value, 1) - depth(value, -2),
        )

    def forward_across(value, halo):
        return (
            across(value, halo, 1) - value,
            across(value, halo, 2) - across(value, halo, -1),
        )

    def backward_across(value, halo):
        return (
            value - across(value, halo, -1),
            across(value, halo, 1) - across(value, halo, -2),
        )

    def forward_strike(ref, comp, slab):
        return (
            ref[comp, slab + 1] - ref[comp, slab],
            ref[comp, slab + 2] - ref[comp, slab - 1],
        )

    def backward_strike(ref, comp, slab):
        return (
            ref[comp, slab] - ref[comp, slab - 1],
            ref[comp, slab + 1] - ref[comp, slab - 2],
        )

    def combine(*pairs):
        near, far = pairs[0]
        for pair in pairs[1:]:
            near, far = near + pair[0], far + pair[1]
        return NEAR * near - FAR * far

    def velocity_slab(x):
        slab = x + 2
        b = buoyancy[x]
        xy, yz, yy = stress[XY, slab], stress[YZ, slab], stress[YY, slab]
        xz, zz = stress[XZ, slab], stress[ZZ, slab]
        velocity[VX, slab] += b * combine(
            forward_strike(stress, XX, slab),
            backward_across(xy, stress_halo[0, x]),
            backward_depth(xz),
        )
        velocity[VY, slab] += b * combine(
            backward_strike(stress, XY, slab),
            forward_across(yy, stress_halo[2, x]),
            backward_depth(yz),
        )
        velocity[VZ, slab] += b * combine(
            backward_strike(stress, XZ, slab),
            backward_across(yz, stress_halo[1, x]),
            forward_depth(zz),
        )

    def stress_slab(x, r):
        slab = x + 2
        mu, la = shear[x], lame[x]
        vx, vy, vz = velocity[VX, slab], velocity[VY, slab], velocity[VZ, slab]
        hx, hz, hy = velocity_halo[0, x], velocity_halo[1, x], velocity_halo[2, x]
        ex = combine(backward_strike(velocity, VX, slab))
        ey = combine(backward_across(vy, hy))
        ez = combine(backward_depth(vz))
        spread = la * (ex + ey + ez)
        twice = 2.0 * mu
        stress[XX, slab] += spread + twice * ex
        stress[YY, slab] += spread + twice * ey
        stress[ZZ, slab] += spread + twice * ez
        sheared = stress[XY, slab] + mu * combine(
            forward_across(vx, hx), forward_strike(velocity, VY, slab)
        )
        stress[XY, slab] = sheared
        trial[pl.ds(r, 1), :] = sheared[0:1]
        stress[XZ, slab] += mu * combine(
            forward_depth(vx), forward_strike(velocity, VZ, slab)
        )
        stress[YZ, slab] += mu * combine(forward_depth(vy), forward_across(vz, hz))

    def outer(i):
        return i + jnp.where(i >= 4, 8, 0)

    def velocity_outer(i, carry):
        velocity_slab(outer(i))
        return carry

    def velocity_inner(i, carry):
        velocity_slab(i + 4)
        return carry

    def stress_outer(i, carry):
        stress_slab(outer(i), i)
        return carry

    def stress_inner(i, carry):
        stress_slab(i + 4, i + 8)
        return carry

    owner = fault_tile[strike]
    is_owner = owner == cross
    strike_of = (0, 1, 2, 3, 12, 13, 14, 15, 4, 5, 6, 7, 8, 9, 10, 11)

    for r, x in enumerate(strike_of):
        fault[0, r : r + 1, :] = shear[x, 0:1, :]
        ratio[r : r + 1, :] = buoyancy[x, 0:1, :]
    fault[0] = 0.5 * jnp.sqrt(fault[0] / ratio[...])

    def unpack():
        for step in range(1, 8):
            pack_copy(step).wait_recv()
        part = lax.broadcasted_iota(jnp.int32, (CX, 128), 1) // 32
        for half in range(2):
            blocks = [packed[4 * half + j] for j in range(4)]
            for index in range(4):
                value = None
                for j in range(4):
                    amount = (32 * (j - index)) % 128
                    moved = pltpu.roll(blocks[j], amount, 1) if amount else blocks[j]
                    value = moved if value is None else jnp.where(part == j, moved, value)
                fault[1 + index, :, 128 * half : 128 * half + 128] = value

    def friction(half):
        rows = slice(8 * half, 8 * half + 8)
        damping, before = fault[0, rows], fault[1, rows]
        a, psi = fault[3, rows], fault[4, rows]
        start_value = trial[rows]
        total = start_value + before
        width = 2.0 * ref_rate * jnp.exp(-psi / a)
        strength = a * fault[2, rows]
        scale = damping * width
        argument = total / scale
        magnitude = jnp.abs(argument)
        log = jnp.log(magnitude + jnp.sqrt(magnitude * magnitude + 1.0))
        u = jnp.where(argument < 0.0, -log, log)
        half_scale = 0.5 * scale
        for _ in range(NEWTON):
            grow, shrink = half_scale * jnp.exp(u), half_scale * jnp.exp(-u)
            u = u - (strength * u + (grow - shrink) - total) / (strength + (grow + shrink))
        slip = width * (0.5 * (jnp.exp(u) - jnp.exp(-u)))
        change = total - damping * slip - before
        fault[4, rows] = psi + evolve_rate * (
            jnp.exp((base_friction - psi) / evolve_b) - jnp.abs(slip) / ref_rate
        )
        fault[5, rows] = slip
        update = jnp.where(is_owner, change, start_value)
        for i in range(8):
            stress[XY, 2 + strike_of[8 * half + i], 0:1, :] = update[i : i + 1]

    def step_body(step, carry):
        wait_recv(stress_strike() + stress_cross(0) + stress_cross(1))

        @pl.when(step > 0)
        def _():
            wait_send(velocity_strike() + velocity_cross(0) + velocity_cross(1))

        lax.fori_loop(0, 8, velocity_outer, 0)
        start(velocity_strike() + velocity_cross(0) + velocity_cross(1))
        wait_recv(stress_cross(2))

        @pl.when(step > 0)
        def _():
            wait_send(velocity_cross(2))

        lax.fori_loop(0, 8, velocity_inner, 0)
        start(velocity_cross(2))

        @pl.when(step == 0)
        def _():
            unpack()

        wait_recv(velocity_strike() + velocity_cross(0) + velocity_cross(1))
        wait_send(stress_strike() + stress_cross(0) + stress_cross(1))
        lax.fori_loop(0, 8, stress_outer, 0)
        friction(0)

        @pl.when(step < STEPS - 1)
        def _():
            start(stress_strike() + stress_cross(0) + stress_cross(1))

        wait_recv(velocity_cross(2))
        wait_send(stress_cross(2))
        lax.fori_loop(0, 8, stress_inner, 0)
        friction(1)

        @pl.when(step < STEPS - 1)
        def _():
            start(stress_cross(2))

        return carry

    lax.fori_loop(0, STEPS, step_body, 0)
    wait_send(velocity_strike() + velocity_cross(0) + velocity_cross(1) + velocity_cross(2))

    for half in range(2):
        for j in range(4):
            lanes = slice(128 * half, 128 * half + 128)
            slip_part, state_part = fault[5, :, lanes], fault[4, :, lanes]
            first = pltpu.roll(slip_part, (128 - 32 * j) % 128, 1) if j else slip_part
            second = pltpu.roll(state_part, (160 - 32 * j) % 128, 1) if j != 1 else state_part
            part = lax.broadcasted_iota(jnp.int32, (CX, 128), 1)
            result[0, 4 * half + j] = jnp.where(part < 32, first, second)

    def result_copy(step):
        other = lax.rem(cross + step, n_cross)
        return pltpu.make_async_remote_copy(
            src_ref=result.at[0, other],
            dst_ref=result.at[1, cross],
            send_sem=result_send.at[step],
            recv_sem=result_recv.at[step],
            device_id=(strike, other),
            device_id_type=MESH,
        )

    for step in range(1, 8):
        result_copy(step).start()
    result[1, cross] = result[0, cross]

    stores = []
    for index, comp in enumerate(STRESS_ORDER):
        stores.append((stress.at[index, pl.ds(2, CX)], stress_out.at[comp]))
    for index, comp in enumerate(VELOCITY_ORDER):
        stores.append((velocity.at[index, pl.ds(2, CX)], velocity_out.at[comp]))
    stores = [
        pltpu.make_async_copy(source, target, store_sem.at[index])
        for index, (source, target) in enumerate(stores)
    ]
    for copy in stores:
        copy.start()
    for step in range(1, 8):
        result_copy(step).wait_recv()
    block = result[1, owner]
    for ref, first in ((slip_out, 0), (state_out, 32)):
        value = block[:, first : first + 32]
        ref[0:4] = value[0:4]
        ref[12:16] = value[4:8]
        ref[4:12] = value[8:16]
    for step in range(1, 8):
        pack_copy(step).wait_send()
        result_copy(step).wait_send()
    for copy in stores:
        copy.wait()


def local(
    velocity, stress, buoyancy, lame, shear, fault_tile, prestress, normal_stress, rate_a, state
):
    anywhere = pl.BlockSpec(memory_space=pl.ANY)
    vmem = pl.BlockSpec(memory_space=pltpu.VMEM)
    smem = pl.BlockSpec(memory_space=pltpu.SMEM)
    f32 = jnp.float32
    return pl.pallas_call(
        wave_kernel,
        out_shape=(
            jax.ShapeDtypeStruct(velocity.shape, f32),
            jax.ShapeDtypeStruct(stress.shape, f32),
            jax.ShapeDtypeStruct(state.shape, f32),
            jax.ShapeDtypeStruct(state.shape, f32),
        ),
        in_specs=[anywhere] * 5 + [smem] + [vmem] * 4,
        out_specs=(anywhere, anywhere, vmem, vmem),
        scratch_shapes=[
            pltpu.VMEM((6, CX + 4, CY, NZ), f32),
            pltpu.VMEM((3, CX + 4, CY, NZ), f32),
            pltpu.VMEM((3, CX, CY, NZ), f32),
            pltpu.VMEM((3, CX, CY, NZ), f32),
            pltpu.VMEM((CX, CY, NZ), f32),
            pltpu.VMEM((CX, CY, NZ), f32),
            pltpu.VMEM((CX, CY, NZ), f32),
            pltpu.VMEM((CX, NZ), f32),
            pltpu.VMEM((CX, NZ), f32),
            pltpu.VMEM((6, CX, NZ), f32),
            pltpu.VMEM((8, CX, 128), f32),
            pltpu.VMEM((2, 8, CX, 128), f32),
            pltpu.SemaphoreType.DMA((2, 16)),
            pltpu.SemaphoreType.DMA((2, 16)),
            pltpu.SemaphoreType.DMA((8,)),
            pltpu.SemaphoreType.DMA((8,)),
            pltpu.SemaphoreType.DMA((8,)),
            pltpu.SemaphoreType.DMA((8,)),
            pltpu.SemaphoreType.DMA((12,)),
            pltpu.SemaphoreType.DMA((9,)),
        ],
        compiler_params=pltpu.CompilerParams(
            collective_id=0, has_side_effects=True, vmem_limit_bytes=48 * 2**20
        ),
    )(
        stress,
        velocity,
        buoyancy,
        lame,
        shear,
        fault_tile,
        prestress,
        normal_stress,
        rate_a,
        state,
    )


def solution(mesh):
    in_specs = (
        P(None, "strike", "cross", None),
        P(None, "strike", "cross", None),
        P("strike", "cross", None),
        P("strike", "cross", None),
        P("strike", "cross", None),
        P(),
        P("strike", "cross"),
        P("strike", "cross"),
        P("strike", "cross"),
        P("strike", "cross"),
    )
    out_specs = (
        P(None, "strike", "cross", None),
        P(None, "strike", "cross", None),
        P("strike", "cross"),
        P("strike", "cross"),
    )
    return jax.shard_map(local, mesh=mesh, in_specs=in_specs, out_specs=out_specs, check_vma=False)
```

time: 475 us -> 81.3 us (0.17)
  the two profiles are of different devices: /device:TPU:32 before, /device:TPU:33 now
where the time goes in v1:
time: 81.3 us; the launch traced here: 80.8 us
  Pallas kernels  68.1 us (84%)
  local copies, waits for them, and re-layouts  12 us (15%)
    pallas_call x1, Pallas kernels, local(): pl.pallas_call(wave_kernel, out_shape=(jax.ShapeDtypeStruct(velocity.shap...  68.1 us
    unnamed x24, local copies, waits for them, and re-layouts  12 us

profile of v1, /device:TPU:33, one launch (start us, length us, event | category | flops | bytes accessed | tf_op | source)
XLA Modules:
  0.0 80.8 jit_solution(14188912803655782864)
XLA Ops:
  0.6 0.0 copy-start
  0.6 1.4 %copy-done = f32[6,16,16,256]{3,2,1,0:T(8,128)S(1)} copy-done((f32[6,16,16,256]{3,2,1,0:T(8,128)S(1)}, f32[6,16,16,256]{3,2,1,0:T(8,128)}, u32[]{:S(2)}) %copy-start) | copy-done | bytes 1572888
  2.0 0.0 copy-start.1
  2.0 1.1 %copy-done.1 = f32[3,16,16,256]{3,2,1,0:T(8,128)S(1)} copy-done((f32[3,16,16,256]{3,2,1,0:T(8,128)S(1)}, f32[3,16,16,256]{3,2,1,0:T(8,128)}, u32[]{:S(2)}) %copy-start.1) | copy-done | bytes 786456
  3.2 0.0 copy-start.2
  3.2 0.9 %copy-done.2 = f32[16,16,256]{2,1,0:T(8,128)S(1)} copy-done((f32[16,16,256]{2,1,0:T(8,128)S(1)}, f32[16,16,256]{2,1,0:T(8,128)}, u32[]{:S(2)}) %copy-start.2) | copy-done | bytes 262168
  4.1 0.0 copy-start.3
  4.1 0.9 %copy-done.3 = f32[16,16,256]{2,1,0:T(8,128)S(1)} copy-done((f32[16,16,256]{2,1,0:T(8,128)S(1)}, f32[16,16,256]{2,1,0:T(8,128)}, u32[]{:S(2)}) %copy-start.3) | copy-done | bytes 262168
  5.1 0.0 copy-start.4
  5.1 0.9 %copy-done.4 = f32[16,16,256]{2,1,0:T(8,128)S(1)} copy-done((f32[16,16,256]{2,1,0:T(8,128)S(1)}, f32[16,16,256]{2,1,0:T(8,128)}, u32[]{:S(2)}) %copy-start.4) | copy-done | bytes 262168
  6.0 0.0 copy-start.5
  6.0 0.7 copy-done.5
  6.7 0.0 copy-start.6
  6.7 0.7 copy-done.6
  7.4 0.0 copy-start.7
  7.4 0.7 copy-done.7
  8.1 0.0 copy-start.8
  8.1 0.7 copy-done.8
  8.8 0.0 copy-start.9
  8.8 0.7 copy-done.9
  9.5 68.1 %shard_map.129 = (f32[3,16,16,256]{3,2,1,0:T(8,128)S(1)}, f32[6,16,16,256]{3,2,1,0:T(8,128)S(1)}, f32[16,32]{1,0:T(8,128)S(1)}, f32[16,32]{1,0:T(8,128)S(1)}) custom-call(f32[6,16,16,256]{3,2,1,0:T(8,128)S(1)} %copy-done, f32[3,16,16,256]{3,2,1,0:T(8,128)S(1)} %copy-done.1, f32[16,16,256]{2,1,0:T(8,128)S(1)} %copy-done.2, f32[16,16,256]{2,1,0:T(8,128)S(1)} %copy-done.3, ...), custom_call_target="tpu_custom_call" | custom-call | tf_op jit(solution)/shard_map/pallas_call | solution.py:523
  77.6 0.9 %copy.18 = f32[3,16,16,256]{3,2,1,0:T(8,128)} copy(f32[3,16,16,256]{3,2,1,0:T(8,128)S(1)} %get-tuple-element.8) | data formatting | bytes 1572864
  78.5 1.1 %copy.19 = f32[6,16,16,256]{3,2,1,0:T(8,128)} copy(f32[6,16,16,256]{3,2,1,0:T(8,128)S(1)} %get-tuple-element.9) | data formatting | bytes 3145728
  79.6 0.6 copy.20
  80.2 0.6 copy.21
Async XLA Ops:
  0.6 1.4 %copy-start = (f32[6,16,16,256]{3,2,1,0:T(8,128)S(1)}, f32[6,16,16,256]{3,2,1,0:T(8,128)}, u32[]{:S(2)}) copy-start(f32[6,16,16,256]{3,2,1,0:T(8,128)} %stress_in.1) | copy-start | bytes 4718596
  2.0 1.1 %copy-start.1 = (f32[3,16,16,256]{3,2,1,0:T(8,128)S(1)}, f32[3,16,16,256]{3,2,1,0:T(8,128)}, u32[]{:S(2)}) copy-start(f32[3,16,16,256]{3,2,1,0:T(8,128)} %velocity_in.1) | copy-start | bytes 2359300
  3.2 0.9 %copy-start.2 = (f32[16,16,256]{2,1,0:T(8,128)S(1)}, f32[16,16,256]{2,1,0:T(8,128)}, u32[]{:S(2)}) copy-start(f32[16,16,256]{2,1,0:T(8,128)} %buoyancy_in.1) | copy-start | bytes 786436
  4.1 0.9 %copy-start.3 = (f32[16,16,256]{2,1,0:T(8,128)S(1)}, f32[16,16,256]{2,1,0:T(8,128)}, u32[]{:S(2)}) copy-start(f32[16,16,256]{2,1,0:T(8,128)} %lame_in.1) | copy-start | bytes 786436
  5.1 0.9 %copy-start.4 = (f32[16,16,256]{2,1,0:T(8,128)S(1)}, f32[16,16,256]{2,1,0:T(8,128)}, u32[]{:S(2)}) copy-start(f32[16,16,256]{2,1,0:T(8,128)} %shear_in.1) | copy-start | bytes 786436
  6.0 0.7 copy-start.5
  6.7 0.7 copy-start.6
  7.4 0.7 copy-start.7
  8.1 0.7 copy-start.8
  8.8 0.7 copy-start.9

commit v2 on v1

--- a/solution.py
+++ b/solution.py
@@ -513,6 +513,17 @@
         copy.wait()
 
 
+def write_kernel(a, b, c, d, a_out, b_out, c_out, d_out, sem):
+    copies = [
+        pltpu.make_async_copy(source, target, sem.at[index])
+        for index, (source, target) in enumerate(((a, a_out), (b, b_out), (c, c_out), (d, d_out)))
+    ]
+    for copy in copies:
+        copy.start()
+    for copy in copies:
+        copy.wait()
+
+
 def local(
     velocity, stress, buoyancy, lame, shear, fault_tile, prestress, normal_stress, rate_a, state
 ):
@@ -520,7 +531,7 @@
     vmem = pl.BlockSpec(memory_space=pltpu.VMEM)
     smem = pl.BlockSpec(memory_space=pltpu.SMEM)
     f32 = jnp.float32
-    return pl.pallas_call(
+    results = pl.pallas_call(
         wave_kernel,
         out_shape=(
             jax.ShapeDtypeStruct(velocity.shape, f32),
@@ -556,17 +567,29 @@
             collective_id=0, has_side_effects=True, vmem_limit_bytes=48 * 2**20
         ),
     )(
-        stress,
-        velocity,
-        buoyancy,
-        lame,
-        shear,
-        fault_tile,
-        prestress,
-        normal_stress,
-        rate_a,
-        state,
+        *[
+            pltpu.with_memory_space_constraint(value, pltpu.HBM)
+            for value in (
+                stress,
+                velocity,
+                buoyancy,
+                lame,
+                shear,
+                fault_tile,
+                prestress,
+                normal_stress,
+                rate_a,
+                state,
+            )
+        ]
     )
+    return pl.pallas_call(
+        write_kernel,
+        out_shape=tuple(jax.ShapeDtypeStruct(value.shape, f32) for value in results),
+        in_specs=[vmem] * 4,
+        out_specs=(anywhere,) * 4,
+        scratch_shapes=[pltpu.SemaphoreType.DMA((4,))],
+    )(*[pltpu.with_memory_space_constraint(value, pltpu.VMEM) for value in results])
 
 
 def solution(mesh):

time: 81.3 us -> 69.3 us (0.85)
  local copies, waits for them, and re-layouts: 12 us -> 0 us
    unnamed x24 -> x0, local copies, waits for them, and re-layouts: 12 us -> none
    pallas_call x0 -> x1, Pallas kernels: none -> 1.44 us  [local(): pl.pallas_call(write_kernel, out_shape=tuple((jax.ShapeDtypeStruct(value....]
    pallas_call x1, Pallas kernels: 68.1 us -> 67.1 us  [local(): pl.pallas_call(wave_kernel, out_shape=(jax.ShapeDtypeStruct(velocity.shap...]
where the time goes in v2:
time: 69.3 us; the launch traced here: 69.2 us
  Pallas kernels  68.5 us (99%)
    pallas_call x1, Pallas kernels, local(): pl.pallas_call(wave_kernel, out_shape=(jax.ShapeDtypeStruct(velocity.shap...  67.1 us
    pallas_call x1, Pallas kernels, local(): pl.pallas_call(write_kernel, out_shape=tuple((jax.ShapeDtypeStruct(value....  1.44 us

profile of v2, /device:TPU:33, one launch (start us, length us, event | category | flops | bytes accessed | tf_op | source)
XLA Modules:
  0.0 69.2 jit_solution(1844685026331681515)
XLA Ops:
  0.6 67.1 %shard_map.129 = (f32[3,16,16,256]{3,2,1,0:T(8,128)S(1)}, f32[6,16,16,256]{3,2,1,0:T(8,128)S(1)}, f32[16,32]{1,0:T(8,128)S(1)}, f32[16,32]{1,0:T(8,128)S(1)}) custom-call(f32[6,16,16,256]{3,2,1,0:T(8,128)} %stress_in.1, f32[3,16,16,256]{3,2,1,0:T(8,128)} %velocity_in.1, f32[16,16,256]{2,1,0:T(8,128)} %buoyancy_in.1, f32[16,16,256]{2,1,0:T(8,128)} %lame_in.1, ...), custom_call_target="tpu_custom_call" | custom-call | tf_op jit(solution)/shard_map/pallas_call | solution.py:534
  67.7 1.4 %shard_map.130 = (f32[3,16,16,256]{3,2,1,0:T(8,128)}, f32[6,16,16,256]{3,2,1,0:T(8,128)}, f32[16,32]{1,0:T(8,128)}, f32[16,32]{1,0:T(8,128)}) custom-call(f32[3,16,16,256]{3,2,1,0:T(8,128)S(1)} %get-tuple-element.8.a, f32[6,16,16,256]{3,2,1,0:T(8,128)S(1)} %get-tuple-element.9.b, f32[16,32]{1,0:T(8,128)S(1)} %get-tuple-element.10.c, ...), custom_call_target="tpu_custom_call" | custom-call | tf_op jit(solution)/shard_map/pallas_call | solution.py:586

commit v3 on v2

--- a/solution.py
+++ b/solution.py
@@ -14,6 +14,7 @@
 base_friction = 0.6
 evolve_b = 0.03
 
+UNROLL = 3
 CX = 16
 CY = 16
 NZ = 256
@@ -27,7 +28,20 @@
 NEAR = step_ratio * 1.125
 FAR = step_ratio / 24.0
 
-RUNS = ((0, 4), (12, 4), (4, 8))
+INNER_RUNS = ((2, 6), (8, 6))
+RUNS = ((0, 2), (14, 2)) + INNER_RUNS
+COPIES = 6 + 4 * len(RUNS)
+
+EDGE_ROWS = tuple(zip((0, 1, 2, 3), (0, 1, 14, 15)))
+BASES = []
+FAULT_ROWS = 8
+for _first, _count in INNER_RUNS:
+    BASES.append(FAULT_ROWS)
+    FAULT_ROWS += -(-_count // 8) * 8
+INNER_ROWS = tuple(
+    tuple((base + i, first + i) for i in range(count))
+    for base, (first, count) in zip(BASES, INNER_RUNS)
+)
 
 
 def wave_kernel(
@@ -55,6 +69,7 @@
     trial,
     ratio,
     fault,
+    ordered,
     packed,
     result,
     send_sem,
@@ -114,11 +129,7 @@
     lax.fori_loop(0, CX, clear, 0)
 
     for index, ref in enumerate((prestress, normal_stress, rate_a, state)):
-        value = ref[...]
-        columns = pl.ds(32 * index, 32)
-        packed[cross, 0:4, columns] = value[0:4]
-        packed[cross, 4:8, columns] = value[12:16]
-        packed[cross, 8:16, columns] = value[4:12]
+        packed[cross, :, pl.ds(32 * index, 32)] = ref[...]
 
     barrier = pltpu.get_barrier_semaphore()
     for side in ("up", "down"):
@@ -149,10 +160,12 @@
 
     def stress_strike():
         return [
-            remote(0, 0, "up", stress.at[1:3, 16:18], stress.at[1:3, 0:2]),
-            remote(0, 1, "up", stress.at[0:1, 17:18], stress.at[0:1, 1:2]),
-            remote(0, 2, "down", stress.at[1:3, 2:3], stress.at[1:3, 18:19]),
-            remote(0, 3, "down", stress.at[0:1, 2:4], stress.at[0:1, 18:20]),
+            remote(0, 0, "up", stress.at[XZ, 16:18], stress.at[XZ, 0:2]),
+            remote(0, 1, "up", stress.at[XX, 17:18], stress.at[XX, 1:2]),
+            remote(0, 2, "down", stress.at[XZ, 2:3], stress.at[XZ, 18:19]),
+            remote(0, 3, "down", stress.at[XX, 2:4], stress.at[XX, 18:20]),
+            remote(0, 4, "up", stress.at[XY, 16:18], stress.at[XY, 0:2]),
+            remote(0, 5, "down", stress.at[XY, 2:3], stress.at[XY, 18:19]),
         ]
 
     def velocity_strike():
@@ -166,7 +179,7 @@
     def stress_cross(run):
         first, count = RUNS[run]
         own, halo = pl.ds(2 + first, count), pl.ds(first, count)
-        base = 4 + 4 * run
+        base = 6 + 4 * run
         return [
             remote(
                 0, base, "right", stress.at[2:4, own, 14:16], stress_halo.at[0:2, halo, 14:16]
@@ -185,7 +198,7 @@
     def velocity_cross(run):
         first, count = RUNS[run]
         own, halo = pl.ds(2 + first, count), pl.ds(first, count)
-        base = 4 + 4 * run
+        base = 6 + 4 * run
         return [
             remote(
                 1, base, "right", velocity.at[2:3, own, 14:16], velocity_halo.at[2:3, halo, 14:16]
@@ -228,7 +241,9 @@
 
     for copy in loads[:6]:
         copy.wait()
-    start(stress_strike() + stress_cross(0) + stress_cross(1) + stress_cross(2))
+    start(stress_strike() + stress_cross(0) + stress_cross(1))
+    wait_send(stress_strike() + stress_cross(0) + stress_cross(1))
+    start([c for run in range(2, len(RUNS)) for c in stress_cross(run)])
 
     def pack_copy(step):
         other = lax.rem(cross + step, n_cross)
@@ -247,135 +262,180 @@
     for copy in loads[6:]:
         copy.wait()
 
-    row = lax.broadcasted_iota(jnp.int32, (CY, NZ), 0)
-    lane = lax.broadcasted_iota(jnp.int32, (CY, NZ), 1)
-
-    def depth(value, offset):
-        moved = pltpu.roll(value, (-offset) % NZ, 1)
+    row = lax.broadcasted_iota(jnp.int32, (8, 128), 0)
+    lane = lax.broadcasted_iota(jnp.int32, (8, 128), 1)
+    nothing = jnp.zeros((8, 128), jnp.float32)
+
+    def tile(ref, index, slab, a, b):
+        return ref[index, slab, 8 * a : 8 * a + 8, 128 * b : 128 * b + 128]
+
+    def tiles(ref, index, slab):
+        return [[tile(ref, index, slab, a, b) for b in range(2)] for a in range(2)]
+
+    def move(here, beside, offset, axis, size):
+        place = row if axis == 0 else lane
         if offset < 0:
-            return jnp.where(lane < -offset, 0.0, moved)
-        return jnp.where(lane >= NZ - offset, 0.0, moved)
-
-    def across(value, halo, offset):
-        if offset < 0:
-            joined = jnp.where(row >= CY + offset, halo, value)
+            joined = jnp.where(place >= size + offset, beside, here)
         else:
-            joined = jnp.where(row < offset, halo, value)
-        return pltpu.roll(joined, (-offset) % CY, 0)
-
-    def forward_depth(value):
+            joined = jnp.where(place < offset, beside, here)
+        return pltpu.roll(joined, (-offset) % size, axis)
+
+    def depth(field, a, b, offset):
+        other = b + (1 if offset > 0 else -1)
+        beside = field[a][other] if 0 <= other < 2 else nothing
+        return move(field[a][b], beside, offset, 1, 128)
+
+    def across(field, a, b, offset):
+        other = a + (1 if offset > 0 else -1)
+        beside = field[other][b] if 0 <= other < 2 else field[2][other % 2][b]
+        return move(field[a][b], beside, offset, 0, 8)
+
+    def forward(shift, field, a, b):
+        here = field[a][b]
         return (
-            depth(value, 1) - value,
-            depth(value, 2) - depth(value, -1),
+            shift(field, a, b, 1) - here,
+            shift(field, a, b, 2) - shift(field, a, b, -1),
         )
 
-    def backward_depth(value):
+    def backward(shift, field, a, b):
+        here = field[a][b]
         return (
-            value - depth(value, -1),
-            depth(value, 1) - depth(value, -2),
+            here - shift(field, a, b, -1),
+            shift(field, a, b, 1) - shift(field, a, b, -2),
         )
 
-    def forward_across(value, halo):
+    def forward_strike(ref, index, slab, here, a, b):
         return (
-            across(value, halo, 1) - value,
-            across(value, halo, 2) - across(value, halo, -1),
+            tile(ref, index, slab + 1, a, b) - here,
+            tile(ref, index, slab + 2, a, b) - tile(ref, index, slab - 1, a, b),
         )
 
-    def backward_across(value, halo):
+    def backward_strike(ref, index, slab, here, a, b):
         return (
-            value - across(value, halo, -1),
-            across(value, halo, 1) - across(value, halo, -2),
-        )
-
-    def forward_strike(ref, comp, slab):
-        return (
-            ref[comp, slab + 1] - ref[comp, slab],
-            ref[comp, slab + 2] - ref[comp, slab - 1],
-        )
-
-    def backward_strike(ref, comp, slab):
-        return (
-            ref[comp, slab] - ref[comp, slab - 1],
-            ref[comp, slab + 1] - ref[comp, slab - 2],
+            here - tile(ref, index, slab - 1, a, b),
+            tile(ref, index, slab + 1, a, b) - tile(ref, index, slab - 2, a, b),
         )
 
     def combine(*pairs):
         near, far = pairs[0]
         for pair in pairs[1:]:
             near, far = near + pair[0], far + pair[1]
-        return NEAR * near - FAR * far
+        return near - (FAR / NEAR) * far
 
     def velocity_slab(x):
         slab = x + 2
-        b = buoyancy[x]
-        xy, yz, yy = stress[XY, slab], stress[YZ, slab], stress[YY, slab]
-        xz, zz = stress[XZ, slab], stress[ZZ, slab]
-        velocity[VX, slab] += b * combine(
-            forward_strike(stress, XX, slab),
-            backward_across(xy, stress_halo[0, x]),
-            backward_depth(xz),
-        )
-        velocity[VY, slab] += b * combine(
-            backward_strike(stress, XY, slab),
-            forward_across(yy, stress_halo[2, x]),
-            backward_depth(yz),
-        )
-        velocity[VZ, slab] += b * combine(
-            backward_strike(stress, XZ, slab),
-            backward_across(yz, stress_halo[1, x]),
-            forward_depth(zz),
-        )
+        xx, yy, zz = (tiles(stress, index, slab) for index in (XX, YY, ZZ))
+        xy, xz, yz = (tiles(stress, index, slab) for index in (XY, XZ, YZ))
+        xy.append(tiles(stress_halo, 0, x))
+        yz.append(tiles(stress_halo, 1, x))
+        yy.append(tiles(stress_halo, 2, x))
+        results = []
+        for a in range(2):
+            for b in range(2):
+                factor = NEAR * buoyancy[x, 8 * a : 8 * a + 8, 128 * b : 128 * b + 128]
+                rate_x = combine(
+                    forward_strike(stress, XX, slab, xx[a][b], a, b),
+                    backward(across, xy, a, b),
+                    backward(depth, xz, a, b),
+                )
+                rate_y = combine(
+                    backward_strike(stress, XY, slab, xy[a][b], a, b),
+                    forward(across, yy, a, b),
+                    backward(depth, yz, a, b),
+                )
+                rate_z = combine(
+                    backward_strike(stress, XZ, slab, xz[a][b], a, b),
+                    backward(across, yz, a, b),
+                    forward(depth, zz, a, b),
+                )
+                for index, rate in ((VX, rate_x), (VY, rate_y), (VZ, rate_z)):
+                    results.append((index, a, b, tile(velocity, index, slab, a, b) + factor * rate))
+        for index, a, b, value in results:
+            velocity[index, slab, 8 * a : 8 * a + 8, 128 * b : 128 * b + 128] = value
 
     def stress_slab(x, r):
         slab = x + 2
-        mu, la = shear[x], lame[x]
-        vx, vy, vz = velocity[VX, slab], velocity[VY, slab], velocity[VZ, slab]
-        hx, hz, hy = velocity_halo[0, x], velocity_halo[1, x], velocity_halo[2, x]
-        ex = combine(backward_strike(velocity, VX, slab))
-        ey = combine(backward_across(vy, hy))
-        ez = combine(backward_depth(vz))
-        spread = la * (ex + ey + ez)
-        twice = 2.0 * mu
-        stress[XX, slab] += spread + twice * ex
-        stress[YY, slab] += spread + twice * ey
-        stress[ZZ, slab] += spread + twice * ez
-        sheared = stress[XY, slab] + mu * combine(
-            forward_across(vx, hx), forward_strike(velocity, VY, slab)
-        )
-        stress[XY, slab] = sheared
-        trial[pl.ds(r, 1), :] = sheared[0:1]
-        stress[XZ, slab] += mu * combine(
-            forward_depth(vx), forward_strike(velocity, VZ, slab)
-        )
-        stress[YZ, slab] += mu * combine(forward_depth(vy), forward_across(vz, hz))
+        vx, vy, vz = (tiles(velocity, index, slab) for index in (VX, VY, VZ))
+        vx.append(tiles(velocity_halo, 0, x))
+        vz.append(tiles(velocity_halo, 1, x))
+        vy.append(tiles(velocity_halo, 2, x))
+        results = []
+        for a in range(2):
+            for b in range(2):
+                mu = NEAR * shear[x, 8 * a : 8 * a + 8, 128 * b : 128 * b + 128]
+                la = NEAR * lame[x, 8 * a : 8 * a + 8, 128 * b : 128 * b + 128]
+                ex = combine(backward_strike(velocity, VX, slab, vx[a][b], a, b))
+                ey = combine(backward(across, vy, a, b))
+                ez = combine(backward(depth, vz, a, b))
+                spread = la * (ex + ey + ez)
+                twice = mu + mu
+                changes = (
+                    (XX, spread + twice * ex),
+                    (YY, spread + twice * ey),
+                    (ZZ, spread + twice * ez),
+                    (
+                        XY,
+                        mu
+                        * combine(
+                            forward(across, vx, a, b),
+                            forward_strike(velocity, VY, slab, vy[a][b], a, b),
+                        ),
+                    ),
+                    (
+                        XZ,
+                        mu
+                        * combine(
+                            forward(depth, vx, a, b),
+                            forward_strike(velocity, VZ, slab, vz[a][b], a, b),
+                        ),
+                    ),
+                    (YZ, mu * combine(forward(depth, vy, a, b), forward(across, vz, a, b))),
+                )
+                for index, change in changes:
+                    results.append((index, a, b, tile(stress, index, slab, a, b) + change))
+        for index, a, b, value in results:
+            stress[index, slab, 8 * a : 8 * a + 8, 128 * b : 128 * b + 128] = value
+        first = [value[0:1] for index, a, b, value in results if index == XY and a == 0]
+        trial[pl.ds(r, 1), :] = jnp.concatenate(first, axis=1)
 
     def outer(i):
-        return i + jnp.where(i >= 4, 8, 0)
+        return i + jnp.where(i >= 2, 12, 0)
 
     def velocity_outer(i, carry):
         velocity_slab(outer(i))
         return carry
 
-    def velocity_inner(i, carry):
-        velocity_slab(i + 4)
-        return carry
-
     def stress_outer(i, carry):
         stress_slab(outer(i), i)
         return carry
 
-    def stress_inner(i, carry):
-        stress_slab(i + 4, i + 8)
-        return carry
+    def velocity_inner(run):
+        first, count = INNER_RUNS[run]
+
+        def body(i, carry):
+            velocity_slab(i + first)
+            return carry
+
+        lax.fori_loop(0, count, body, 0, unroll=UNROLL)
+
+    def stress_inner(run):
+        first, count = INNER_RUNS[run]
+
+        def body(i, carry):
+            stress_slab(i + first, i + BASES[run])
+            return carry
+
+        lax.fori_loop(0, count, body, 0, unroll=UNROLL)
 
     owner = fault_tile[strike]
     is_owner = owner == cross
-    strike_of = (0, 1, 2, 3, 12, 13, 14, 15, 4, 5, 6, 7, 8, 9, 10, 11)
-
-    for r, x in enumerate(strike_of):
+
+    for r, x in EDGE_ROWS + sum(INNER_ROWS, ()):
         fault[0, r : r + 1, :] = shear[x, 0:1, :]
         ratio[r : r + 1, :] = buoyancy[x, 0:1, :]
-    fault[0] = 0.5 * jnp.sqrt(fault[0] / ratio[...])
+    for cells in (EDGE_ROWS,) + INNER_ROWS:
+        rows = slice(cells[0][0], cells[-1][0] + 1)
+        fault[0, rows] = 0.5 * jnp.sqrt(fault[0, rows] / ratio[rows])
 
     def unpack():
         for step in range(1, 8):
@@ -389,10 +449,15 @@
                     amount = (32 * (j - index)) % 128
                     moved = pltpu.roll(blocks[j], amount, 1) if amount else blocks[j]
                     value = moved if value is None else jnp.where(part == j, moved, value)
-                fault[1 + index, :, 128 * half : 128 * half + 128] = value
-
-    def friction(half):
-        rows = slice(8 * half, 8 * half + 8)
+                lanes = slice(128 * half, 128 * half + 128)
+                fault[1 + index, 0:2, lanes] = value[0:2]
+                fault[1 + index, 2:4, lanes] = value[14:16]
+                for base, (first, count) in zip(BASES, INNER_RUNS):
+                    fault[1 + index, base : base + count, lanes] = value[first : first + count]
+
+    def friction(cells):
+        first = cells[0][0]
+        rows = slice(first, first + len(cells))
         damping, before = fault[0, rows], fault[1, rows]
         a, psi = fault[3, rows], fault[4, rows]
         start_value = trial[rows]
@@ -415,58 +480,82 @@
         )
         fault[5, rows] = slip
         update = jnp.where(is_owner, change, start_value)
-        for i in range(8):
-            stress[XY, 2 + strike_of[8 * half + i], 0:1, :] = update[i : i + 1]
+        for r, x in cells:
+            stress[XY, 2 + x, 0:1, :] = update[r - first : r - first + 1]
+
+    def split(along, over):
+        free, tied = along[:4], along[4:]
+        for index, copy in enumerate(over):
+            (tied if index % 4 == 2 else free).append(copy)
+        return free, tied
 
     def step_body(step, carry):
         wait_recv(stress_strike() + stress_cross(0) + stress_cross(1))
 
-        @pl.when(step > 0)
-        def _():
-            wait_send(velocity_strike() + velocity_cross(0) + velocity_cross(1))
-
-        lax.fori_loop(0, 8, velocity_outer, 0)
+        lax.fori_loop(0, 4, velocity_outer, 0, unroll=2)
         start(velocity_strike() + velocity_cross(0) + velocity_cross(1))
-        wait_recv(stress_cross(2))
-
-        @pl.when(step > 0)
-        def _():
-            wait_send(velocity_cross(2))
-
-        lax.fori_loop(0, 8, velocity_inner, 0)
-        start(velocity_cross(2))
+        for run in range(len(INNER_RUNS)):
+            wait_recv(stress_cross(2 + run))
+
+            @pl.when(step > 0)
+            def _(run=run):
+                wait_send(velocity_cross(2 + run))
+
+            velocity_inner(run)
+            if run == 0:
+                wait_send(velocity_strike() + velocity_cross(0) + velocity_cross(1))
+            start(velocity_cross(2 + run))
 
         @pl.when(step == 0)
         def _():
             unpack()
 
         wait_recv(velocity_strike() + velocity_cross(0) + velocity_cross(1))
-        wait_send(stress_strike() + stress_cross(0) + stress_cross(1))
-        lax.fori_loop(0, 8, stress_outer, 0)
-        friction(0)
+        lax.fori_loop(0, 4, stress_outer, 0, unroll=2)
+        free, tied = split(stress_strike(), stress_cross(0) + stress_cross(1))
 
         @pl.when(step < STEPS - 1)
         def _():
-            start(stress_strike() + stress_cross(0) + stress_cross(1))
-
-        wait_recv(velocity_cross(2))
-        wait_send(stress_cross(2))
-        lax.fori_loop(0, 8, stress_inner, 0)
-        friction(1)
+            start(free)
+
+        friction(EDGE_ROWS)
 
         @pl.when(step < STEPS - 1)
         def _():
-            start(stress_cross(2))
+            start(tied)
+
+        for run in range(len(INNER_RUNS)):
+            wait_recv(velocity_cross(2 + run))
+            wait_send(stress_cross(2 + run))
+            stress_inner(run)
+            free, tied = split([], stress_cross(2 + run))
+
+            @pl.when(step < STEPS - 1)
+            def _(free=free, run=run):
+                if run == 0:
+                    wait_send(stress_strike() + stress_cross(0) + stress_cross(1))
+                start(free)
+
+            friction(INNER_ROWS[run])
+
+            @pl.when(step < STEPS - 1)
+            def _(tied=tied):
+                start(tied)
 
         return carry
 
     lax.fori_loop(0, STEPS, step_body, 0)
-    wait_send(velocity_strike() + velocity_cross(0) + velocity_cross(1) + velocity_cross(2))
-
+    wait_send([c for run in range(2, len(RUNS)) for c in velocity_cross(run)])
+
+    for index, which in enumerate((5, 4)):
+        ordered[index, 0:2] = fault[which, 0:2]
+        ordered[index, 14:16] = fault[which, 2:4]
+        for base, (first, count) in zip(BASES, INNER_RUNS):
+            ordered[index, first : first + count] = fault[which, base : base + count]
     for half in range(2):
         for j in range(4):
             lanes = slice(128 * half, 128 * half + 128)
-            slip_part, state_part = fault[5, :, lanes], fault[4, :, lanes]
+            slip_part, state_part = ordered[0, :, lanes], ordered[1, :, lanes]
             first = pltpu.roll(slip_part, (128 - 32 * j) % 128, 1) if j else slip_part
             second = pltpu.roll(state_part, (160 - 32 * j) % 128, 1) if j != 1 else state_part
             part = lax.broadcasted_iota(jnp.int32, (CX, 128), 1)
@@ -502,10 +591,7 @@
         result_copy(step).wait_recv()
     block = result[1, owner]
     for ref, first in ((slip_out, 0), (state_out, 32)):
-        value = block[:, first : first + 32]
-        ref[0:4] = value[0:4]
-        ref[12:16] = value[4:8]
-        ref[4:12] = value[8:16]
+        ref[...] = block[:, first : first + 32]
     for step in range(1, 8):
         pack_copy(step).wait_send()
         result_copy(step).wait_send()
@@ -549,13 +635,14 @@
             pltpu.VMEM((CX, CY, NZ), f32),
             pltpu.VMEM((CX, CY, NZ), f32),
             pltpu.VMEM((CX, CY, NZ), f32),
-            pltpu.VMEM((CX, NZ), f32),
-            pltpu.VMEM((CX, NZ), f32),
-            pltpu.VMEM((6, CX, NZ), f32),
+            pltpu.VMEM((FAULT_ROWS, NZ), f32),
+            pltpu.VMEM((FAULT_ROWS, NZ), f32),
+            pltpu.VMEM((6, FAULT_ROWS, NZ), f32),
+            pltpu.VMEM((2, CX, NZ), f32),
             pltpu.VMEM((8, CX, 128), f32),
             pltpu.VMEM((2, 8, CX, 128), f32),
-            pltpu.SemaphoreType.DMA((2, 16)),
-            pltpu.SemaphoreType.DMA((2, 16)),
+            pltpu.SemaphoreType.DMA((2, COPIES)),
+            pltpu.SemaphoreType.DMA((2, COPIES)),
             pltpu.SemaphoreType.DMA((8,)),
             pltpu.SemaphoreType.DMA((8,)),
             pltpu.SemaphoreType.DMA((8,)),

time: 69.3 us -> 61.9 us (0.89)
  Pallas kernels: 68.5 us -> 60.7 us
    pallas_call x1, Pallas kernels: 67.1 us -> 59.2 us  [local(): pl.pallas_call(wave_kernel, out_shape=(jax.ShapeDtypeStruct(velocity.shap...]
where the time goes in v3:
time: 61.9 us; the launch traced here: 61.3 us
  Pallas kernels  60.7 us (98%)
  between operations  0.64 us (1%)
    pallas_call x1, Pallas kernels, local(): pl.pallas_call(wave_kernel, out_shape=(jax.ShapeDtypeStruct(velocity.shap...  59.2 us
    pallas_call x1, Pallas kernels, local(): pl.pallas_call(write_kernel, out_shape=tuple((jax.ShapeDtypeStruct(value....  1.44 us

profile of v3, /device:TPU:33, one launch (start us, length us, event | category | flops | bytes accessed | tf_op | source)
XLA Modules:
  0.0 61.3 jit_solution(7641330164776253921)
XLA Ops:
  0.6 59.2 %shard_map.129 = (f32[3,16,16,256]{3,2,1,0:T(8,128)S(1)}, f32[6,16,16,256]{3,2,1,0:T(8,128)S(1)}, f32[16,32]{1,0:T(8,128)S(1)}, f32[16,32]{1,0:T(8,128)S(1)}) custom-call(f32[6,16,16,256]{3,2,1,0:T(8,128)} %stress_in.1, f32[3,16,16,256]{3,2,1,0:T(8,128)} %velocity_in.1, f32[16,16,256]{2,1,0:T(8,128)} %buoyancy_in.1, f32[16,16,256]{2,1,0:T(8,128)} %lame_in.1, ...), custom_call_target="tpu_custom_call" | custom-call | tf_op jit(solution)/shard_map/pallas_call | solution.py:620
  59.9 1.4 %shard_map.130 = (f32[3,16,16,256]{3,2,1,0:T(8,128)}, f32[6,16,16,256]{3,2,1,0:T(8,128)}, f32[16,32]{1,0:T(8,128)}, f32[16,32]{1,0:T(8,128)}) custom-call(f32[3,16,16,256]{3,2,1,0:T(8,128)S(1)} %get-tuple-element.8.a, f32[6,16,16,256]{3,2,1,0:T(8,128)S(1)} %get-tuple-element.9.b, f32[16,32]{1,0:T(8,128)S(1)} %get-tuple-element.10.c, ...), custom_call_target="tpu_custom_call" | custom-call | tf_op jit(solution)/shard_map/pallas_call | solution.py:673

commit v4 on v3

--- a/solution.py
+++ b/solution.py
@@ -14,7 +14,6 @@
 base_friction = 0.6
 evolve_b = 0.03
 
-UNROLL = 3
 CX = 16
 CY = 16
 NZ = 256
@@ -28,20 +27,11 @@
 NEAR = step_ratio * 1.125
 FAR = step_ratio / 24.0
 
-INNER_RUNS = ((2, 6), (8, 6))
-RUNS = ((0, 2), (14, 2)) + INNER_RUNS
+RUNS = ((2, 0, 14), (8, 8, 0), (6, 2, 8))
+UNROLLS = (2, 2, 3)
 COPIES = 6 + 4 * len(RUNS)
-
-EDGE_ROWS = tuple(zip((0, 1, 2, 3), (0, 1, 14, 15)))
-BASES = []
-FAULT_ROWS = 8
-for _first, _count in INNER_RUNS:
-    BASES.append(FAULT_ROWS)
-    FAULT_ROWS += -(-_count // 8) * 8
-INNER_ROWS = tuple(
-    tuple((base + i, first + i) for i in range(count))
-    for base, (first, count) in zip(BASES, INNER_RUNS)
-)
+BASES = (0, 8, 16)
+FAULT_ROWS = 24
 
 
 def wave_kernel(
@@ -85,6 +75,9 @@
     cross = lax.axis_index("cross")
     n_strike = lax.axis_size("strike")
     n_cross = lax.axis_size("cross")
+    odd = lax.rem(strike, 2)
+    is_odd = odd == 1
+    first_of = [even + (late - even) * odd for _, even, late in RUNS]
     has = {
         "up": strike + 1 < n_strike,
         "down": strike >= 1,
@@ -177,7 +170,7 @@
         ]
 
     def stress_cross(run):
-        first, count = RUNS[run]
+        first, count = first_of[run], RUNS[run][0]
         own, halo = pl.ds(2 + first, count), pl.ds(first, count)
         base = 6 + 4 * run
         return [
@@ -196,7 +189,7 @@
         ]
 
     def velocity_cross(run):
-        first, count = RUNS[run]
+        first, count = first_of[run], RUNS[run][0]
         own, halo = pl.ds(2 + first, count), pl.ds(first, count)
         base = 6 + 4 * run
         return [
@@ -218,32 +211,44 @@
             ),
         ]
 
-    def start(copies):
+    def start(copies, far=None):
         for side, copy in copies:
 
-            @pl.when(has[side])
+            @pl.when(sending(side, far))
             def _(copy=copy):
                 copy.start()
 
-    def wait_recv(copies):
+    def wait_recv(copies, far=None):
         for side, copy in copies:
 
-            @pl.when(has[opposite[side]])
+            @pl.when(receiving(side, far))
             def _(copy=copy):
                 copy.wait_recv()
 
-    def wait_send(copies):
+    def wait_send(copies, far=None):
         for side, copy in copies:
 
-            @pl.when(has[side])
+            @pl.when(sending(side, far))
             def _(copy=copy):
                 copy.wait_send()
 
+    def sending(side, far):
+        if far is None:
+            return has[side]
+        return jnp.logical_and(has[side], is_odd if far == (side == "up") else odd == 0)
+
+    def receiving(side, far):
+        if far is None:
+            return has[opposite[side]]
+        return jnp.logical_and(
+            has[opposite[side]], is_odd if far == (side == "down") else odd == 0
+        )
+
     for copy in loads[:6]:
         copy.wait()
-    start(stress_strike() + stress_cross(0) + stress_cross(1))
-    wait_send(stress_strike() + stress_cross(0) + stress_cross(1))
-    start([c for run in range(2, len(RUNS)) for c in stress_cross(run)])
+    start(stress_strike() + stress_cross(0) + stress_cross(1) + stress_cross(2))
+    wait_send(stress_strike(), True)
+    wait_send(stress_cross(0))
 
     def pack_copy(step):
         other = lax.rem(cross + step, n_cross)
@@ -398,43 +403,28 @@
         first = [value[0:1] for index, a, b, value in results if index == XY and a == 0]
         trial[pl.ds(r, 1), :] = jnp.concatenate(first, axis=1)
 
-    def outer(i):
-        return i + jnp.where(i >= 2, 12, 0)
-
-    def velocity_outer(i, carry):
-        velocity_slab(outer(i))
-        return carry
-
-    def stress_outer(i, carry):
-        stress_slab(outer(i), i)
-        return carry
-
-    def velocity_inner(run):
-        first, count = INNER_RUNS[run]
-
+    def velocity_run(run):
         def body(i, carry):
-            velocity_slab(i + first)
+            velocity_slab(i + first_of[run])
             return carry
 
-        lax.fori_loop(0, count, body, 0, unroll=UNROLL)
-
-    def stress_inner(run):
-        first, count = INNER_RUNS[run]
-
+        lax.fori_loop(0, RUNS[run][0], body, 0, unroll=UNROLLS[run])
+
+    def stress_run(run):
         def body(i, carry):
-            stress_slab(i + first, i + BASES[run])
+            stress_slab(i + first_of[run], i + BASES[run])
             return carry
 
-        lax.fori_loop(0, count, body, 0, unroll=UNROLL)
+        lax.fori_loop(0, RUNS[run][0], body, 0, unroll=UNROLLS[run])
 
     owner = fault_tile[strike]
     is_owner = owner == cross
 
-    for r, x in EDGE_ROWS + sum(INNER_ROWS, ()):
-        fault[0, r : r + 1, :] = shear[x, 0:1, :]
-        ratio[r : r + 1, :] = buoyancy[x, 0:1, :]
-    for cells in (EDGE_ROWS,) + INNER_ROWS:
-        rows = slice(cells[0][0], cells[-1][0] + 1)
+    for run, base in enumerate(BASES):
+        rows = slice(base, base + RUNS[run][0])
+        for i in range(RUNS[run][0]):
+            fault[0, base + i : base + i + 1, :] = shear[first_of[run] + i, 0:1, :]
+            ratio[base + i : base + i + 1, :] = buoyancy[first_of[run] + i, 0:1, :]
         fault[0, rows] = 0.5 * jnp.sqrt(fault[0, rows] / ratio[rows])
 
     def unpack():
@@ -450,14 +440,14 @@
                     moved = pltpu.roll(blocks[j], amount, 1) if amount else blocks[j]
                     value = moved if value is None else jnp.where(part == j, moved, value)
                 lanes = slice(128 * half, 128 * half + 128)
-                fault[1 + index, 0:2, lanes] = value[0:2]
-                fault[1 + index, 2:4, lanes] = value[14:16]
-                for base, (first, count) in zip(BASES, INNER_RUNS):
-                    fault[1 + index, base : base + count, lanes] = value[first : first + count]
-
-    def friction(cells):
-        first = cells[0][0]
-        rows = slice(first, first + len(cells))
+                for base, (count, even, late) in zip(BASES, RUNS):
+                    fault[1 + index, base : base + count, lanes] = jnp.where(
+                        is_odd, value[late : late + count], value[even : even + count]
+                    )
+
+    def friction(run):
+        count = RUNS[run][0]
+        rows = slice(BASES[run], BASES[run] + count)
         damping, before = fault[0, rows], fault[1, rows]
         a, psi = fault[3, rows], fault[4, rows]
         start_value = trial[rows]
@@ -480,78 +470,78 @@
         )
         fault[5, rows] = slip
         update = jnp.where(is_owner, change, start_value)
-        for r, x in cells:
-            stress[XY, 2 + x, 0:1, :] = update[r - first : r - first + 1]
-
-    def split(along, over):
-        free, tied = along[:4], along[4:]
-        for index, copy in enumerate(over):
-            (tied if index % 4 == 2 else free).append(copy)
-        return free, tied
+        for i in range(count):
+            stress[XY, 2 + first_of[run] + i, 0:1, :] = update[i : i + 1]
+
+    def split(copies):
+        return copies[:2] + copies[3:], copies[2:3]
 
     def step_body(step, carry):
-        wait_recv(stress_strike() + stress_cross(0) + stress_cross(1))
-
-        lax.fori_loop(0, 4, velocity_outer, 0, unroll=2)
-        start(velocity_strike() + velocity_cross(0) + velocity_cross(1))
-        for run in range(len(INNER_RUNS)):
-            wait_recv(stress_cross(2 + run))
-
-            @pl.when(step > 0)
-            def _(run=run):
-                wait_send(velocity_cross(2 + run))
-
-            velocity_inner(run)
-            if run == 0:
-                wait_send(velocity_strike() + velocity_cross(0) + velocity_cross(1))
-            start(velocity_cross(2 + run))
+        for run in range(3):
+            if run < 2:
+                wait_recv(stress_strike(), run == 0)
+            wait_recv(stress_cross(run))
+            if run > 0:
+
+                @pl.when(step > 0)
+                def _(run=run):
+                    if run == 1:
+                        wait_send(velocity_strike(), False)
+                    wait_send(velocity_cross(run))
+
+            velocity_run(run)
+            if run < 2:
+                start(velocity_strike(), run == 0)
+            start(velocity_cross(run))
+            if run == 2:
+                wait_send(velocity_strike(), True)
+                wait_send(velocity_cross(0))
 
         @pl.when(step == 0)
         def _():
             unpack()
 
-        wait_recv(velocity_strike() + velocity_cross(0) + velocity_cross(1))
-        lax.fori_loop(0, 4, stress_outer, 0, unroll=2)
-        free, tied = split(stress_strike(), stress_cross(0) + stress_cross(1))
-
-        @pl.when(step < STEPS - 1)
-        def _():
-            start(free)
-
-        friction(EDGE_ROWS)
-
-        @pl.when(step < STEPS - 1)
-        def _():
-            start(tied)
-
-        for run in range(len(INNER_RUNS)):
-            wait_recv(velocity_cross(2 + run))
-            wait_send(stress_cross(2 + run))
-            stress_inner(run)
-            free, tied = split([], stress_cross(2 + run))
+        for run in range(3):
+            if run < 2:
+                wait_recv(velocity_strike(), run == 0)
+            wait_recv(velocity_cross(run))
+            if run > 0:
+                if run == 1:
+                    wait_send(stress_strike(), False)
+                wait_send(stress_cross(run))
+            stress_run(run)
+            free, tied = split(stress_cross(run))
+            along = stress_strike()
 
             @pl.when(step < STEPS - 1)
-            def _(free=free, run=run):
-                if run == 0:
-                    wait_send(stress_strike() + stress_cross(0) + stress_cross(1))
+            def _(run=run, free=free, along=along):
+                if run < 2:
+                    start(along[:4], run == 0)
                 start(free)
-
-            friction(INNER_ROWS[run])
+                if run == 2:
+                    wait_send(along, True)
+                    wait_send(stress_cross(0))
+
+            friction(run)
 
             @pl.when(step < STEPS - 1)
-            def _(tied=tied):
+            def _(run=run, tied=tied, along=along):
+                if run < 2:
+                    start(along[4:], run == 0)
                 start(tied)
 
         return carry
 
     lax.fori_loop(0, STEPS, step_body, 0)
-    wait_send([c for run in range(2, len(RUNS)) for c in velocity_cross(run)])
+    wait_send(velocity_strike(), False)
+    wait_send(velocity_cross(1) + velocity_cross(2))
 
     for index, which in enumerate((5, 4)):
-        ordered[index, 0:2] = fault[which, 0:2]
-        ordered[index, 14:16] = fault[which, 2:4]
-        for base, (first, count) in zip(BASES, INNER_RUNS):
-            ordered[index, first : first + count] = fault[which, base : base + count]
+        for base, (count, even, late) in zip(BASES, RUNS):
+            value = fault[which, base : base + count]
+            ordered[index, even : even + count] = value
+            ordered[2 + index, late : late + count] = value
+        ordered[index] = jnp.where(is_odd, ordered[2 + index], ordered[index])
     for half in range(2):
         for j in range(4):
             lanes = slice(128 * half, 128 * half + 128)
@@ -638,7 +628,7 @@
             pltpu.VMEM((FAULT_ROWS, NZ), f32),
             pltpu.VMEM((FAULT_ROWS, NZ), f32),
             pltpu.VMEM((6, FAULT_ROWS, NZ), f32),
-            pltpu.VMEM((2, CX, NZ), f32),
+            pltpu.VMEM((4, CX, NZ), f32),
             pltpu.VMEM((8, CX, 128), f32),
             pltpu.VMEM((2, 8, CX, 128), f32),
             pltpu.SemaphoreType.DMA((2, COPIES)),

time: 61.9 us -> 60.3 us (0.974)
  Pallas kernels: 60.7 us -> 58.7 us
    pallas_call x1, Pallas kernels: 59.2 us -> 57.2 us  [local(): pl.pallas_call(wave_kernel, out_shape=(jax.ShapeDtypeStruct(velocity.shap...]
where the time goes in v4:
time: 60.3 us; the launch traced here: 59.3 us
  Pallas kernels  58.7 us (97%)
  between operations  0.64 us (1%)
    pallas_call x1, Pallas kernels, local(): pl.pallas_call(wave_kernel, out_shape=(jax.ShapeDtypeStruct(velocity.shap...  57.2 us
    pallas_call x1, Pallas kernels, local(): pl.pallas_call(write_kernel, out_shape=tuple((jax.ShapeDtypeStruct(value....  1.44 us

profile of v4, /device:TPU:33, one launch (start us, length us, event | category | flops | bytes accessed | tf_op | source)
XLA Modules:
  0.0 59.3 jit_solution(2529817415076964061)
XLA Ops:
  0.6 57.2 %shard_map.129 = (f32[3,16,16,256]{3,2,1,0:T(8,128)S(1)}, f32[6,16,16,256]{3,2,1,0:T(8,128)S(1)}, f32[16,32]{1,0:T(8,128)S(1)}, f32[16,32]{1,0:T(8,128)S(1)}) custom-call(f32[6,16,16,256]{3,2,1,0:T(8,128)} %stress_in.1, f32[3,16,16,256]{3,2,1,0:T(8,128)} %velocity_in.1, f32[16,16,256]{2,1,0:T(8,128)} %buoyancy_in.1, f32[16,16,256]{2,1,0:T(8,128)} %lame_in.1, ...), custom_call_target="tpu_custom_call" | custom-call | tf_op jit(solution)/shard_map/pallas_call | solution.py:610
  57.9 1.4 %shard_map.130 = (f32[3,16,16,256]{3,2,1,0:T(8,128)}, f32[6,16,16,256]{3,2,1,0:T(8,128)}, f32[16,32]{1,0:T(8,128)}, f32[16,32]{1,0:T(8,128)}) custom-call(f32[3,16,16,256]{3,2,1,0:T(8,128)S(1)} %get-tuple-element.8.a, f32[6,16,16,256]{3,2,1,0:T(8,128)S(1)} %get-tuple-element.9.b, f32[16,32]{1,0:T(8,128)S(1)} %get-tuple-element.10.c, ...), custom_call_target="tpu_custom_call" | custom-call | tf_op jit(solution)/shard_map/pallas_call | solution.py:663

commit v5 on v4

--- a/solution.py
+++ b/solution.py
@@ -261,9 +261,6 @@
             device_id_type=MESH,
         )
 
-    for step in range(1, 8):
-        pack_copy(step).start()
-
     for copy in loads[6:]:
         copy.wait()
 
@@ -493,13 +490,16 @@
             if run < 2:
                 start(velocity_strike(), run == 0)
             start(velocity_cross(run))
+            if run == 0:
+
+                @pl.when(step == 0)
+                def _():
+                    for other in range(1, 8):
+                        pack_copy(other).start()
+
             if run == 2:
                 wait_send(velocity_strike(), True)
                 wait_send(velocity_cross(0))
-
-        @pl.when(step == 0)
-        def _():
-            unpack()
 
         for run in range(3):
             if run < 2:
@@ -522,6 +522,12 @@
                     wait_send(along, True)
                     wait_send(stress_cross(0))
 
+            if run == 0:
+
+                @pl.when(step == 0)
+                def _():
+                    unpack()
+
             friction(run)
 
             @pl.when(step < STEPS - 1)
@@ -545,11 +551,14 @@
     for half in range(2):
         for j in range(4):
             lanes = slice(128 * half, 128 * half + 128)
-            slip_part, state_part = ordered[0, :, lanes], ordered[1, :, lanes]
-            first = pltpu.roll(slip_part, (128 - 32 * j) % 128, 1) if j else slip_part
-            second = pltpu.roll(state_part, (160 - 32 * j) % 128, 1) if j != 1 else state_part
-            part = lax.broadcasted_iota(jnp.int32, (CX, 128), 1)
-            result[0, 4 * half + j] = jnp.where(part < 32, first, second)
+            part = lax.broadcasted_iota(jnp.int32, (8, 128), 1) // 32
+            value = None
+            for index in range(4):
+                piece = ordered[index // 2, 8 * (index % 2) : 8 * (index % 2) + 8, lanes]
+                amount = (32 * (index - j)) % 128
+                moved = pltpu.roll(piece, amount, 1) if amount else piece
+                value = moved if value is None else jnp.where(part == index, moved, value)
+            result[0, 4 * half + j] = value
 
     def result_copy(step):
         other = lax.rem(cross + step, n_cross)
@@ -580,8 +589,9 @@
     for step in range(1, 8):
         result_copy(step).wait_recv()
     block = result[1, owner]
-    for ref, first in ((slip_out, 0), (state_out, 32)):
-        ref[...] = block[:, first : first + 32]
+    for ref, first in ((slip_out, 0), (state_out, 64)):
+        ref[0:8] = block[:, first : first + 32]
+        ref[8:16] = block[:, first + 32 : first + 64]
     for step in range(1, 8):
         pack_copy(step).wait_send()
         result_copy(step).wait_send()
@@ -590,9 +600,12 @@
 
 
 def write_kernel(a, b, c, d, a_out, b_out, c_out, d_out, sem):
+    pairs = [(b.at[index], b_out.at[index]) for index in range(6)]
+    pairs += [(a.at[index], a_out.at[index]) for index in range(3)]
+    pairs += [(c, c_out), (d, d_out)]
     copies = [
         pltpu.make_async_copy(source, target, sem.at[index])
-        for index, (source, target) in enumerate(((a, a_out), (b, b_out), (c, c_out), (d, d_out)))
+        for index, (source, target) in enumerate(pairs)
     ]
     for copy in copies:
         copy.start()
@@ -630,7 +643,7 @@
             pltpu.VMEM((6, FAULT_ROWS, NZ), f32),
             pltpu.VMEM((4, CX, NZ), f32),
             pltpu.VMEM((8, CX, 128), f32),
-            pltpu.VMEM((2, 8, CX, 128), f32),
+            pltpu.VMEM((2, 8, 8, 128), f32),
             pltpu.SemaphoreType.DMA((2, COPIES)),
             pltpu.SemaphoreType.DMA((2, COPIES)),
             pltpu.SemaphoreType.DMA((8,)),
@@ -665,7 +678,7 @@
         out_shape=tuple(jax.ShapeDtypeStruct(value.shape, f32) for value in results),
         in_specs=[vmem] * 4,
         out_specs=(anywhere,) * 4,
-        scratch_shapes=[pltpu.SemaphoreType.DMA((4,))],
+        scratch_shapes=[pltpu.SemaphoreType.DMA((11,))],
     )(*[pltpu.with_memory_space_constraint(value, pltpu.VMEM) for value in results])
 
 

time: 60.3 us -> 60.3 us (level)
  the two profiles are of different devices: /device:TPU:33 before, /device:TPU:161 now
where the time goes in v5:
time: 60.3 us; the launch traced here: 60.2 us
  Pallas kernels  59.5 us (99%)
  between operations  0.64 us (1%)
    pallas_call x1, Pallas kernels, local(): pl.pallas_call(wave_kernel, out_shape=(jax.ShapeDtypeStruct(velocity.shap...  58 us
    pallas_call x1, Pallas kernels, local(): pl.pallas_call(write_kernel, out_shape=tuple((jax.ShapeDtypeStruct(value....  1.49 us

profile of v5, /device:TPU:161, one launch (start us, length us, event | category | flops | bytes accessed | tf_op | source)
XLA Modules:
  0.0 60.2 jit_solution(635570492593672662)
XLA Ops:
  0.6 58.0 %shard_map.129 = (f32[3,16,16,256]{3,2,1,0:T(8,128)S(1)}, f32[6,16,16,256]{3,2,1,0:T(8,128)S(1)}, f32[16,32]{1,0:T(8,128)S(1)}, f32[16,32]{1,0:T(8,128)S(1)}) custom-call(f32[6,16,16,256]{3,2,1,0:T(8,128)} %stress_in.1, f32[3,16,16,256]{3,2,1,0:T(8,128)} %velocity_in.1, f32[16,16,256]{2,1,0:T(8,128)} %buoyancy_in.1, f32[16,16,256]{2,1,0:T(8,128)} %lame_in.1, ...), custom_call_target="tpu_custom_call" | custom-call | tf_op jit(solution)/shard_map/pallas_call | solution.py:623
  58.7 1.5 %shard_map.130 = (f32[3,16,16,256]{3,2,1,0:T(8,128)}, f32[6,16,16,256]{3,2,1,0:T(8,128)}, f32[16,32]{1,0:T(8,128)}, f32[16,32]{1,0:T(8,128)}) custom-call(f32[3,16,16,256]{3,2,1,0:T(8,128)S(1)} %get-tuple-element.8.a, f32[6,16,16,256]{3,2,1,0:T(8,128)S(1)} %get-tuple-element.9.b, f32[16,32]{1,0:T(8,128)S(1)} %get-tuple-element.10.c, ...), custom_call_target="tpu_custom_call" | custom-call | tf_op jit(solution)/shard_map/pallas_call | solution.py:676
